TPU v7x, 256 devices: a whole 4x4x8 slice. The times are simulated.
256 devices in a mesh: section: 8 (over x, y_hi), fsdp: 32 (over y_lo, z, core).
Axes of the slice: x: 4, y: 4 (y_hi: 2, y_lo: 2; y = y_hi * 2 + y_lo), z: 8, core: 2. Of those that a mesh axis runs over, the one named last changes fastest.
Arguments:
- fwd_first: bfloat16 [8, 3584, 3072], P('section', 'fsdp'), may hold values from -6 to 6
- fwd_second: bfloat16 [8, 3584, 3072], P('section', 'fsdp'), may hold values from -6 to 6
- bwd_first: bfloat16 [8, 3584, 3072], P('section', 'fsdp'), may hold values from -6 to 6
- bwd_second: bfloat16 [8, 3584, 3072], P('section', 'fsdp'), may hold values from -6 to 6
- grad_first: bfloat16 [8, 3584, 3072], P('section', 'fsdp'), may hold values from -6 to 6
- grad_second: bfloat16 [8, 3584, 3072], P('section', 'fsdp'), may hold values from -6 to 6
- w_query: bfloat16 [8, 3072, 256], P('section', 'fsdp'), may hold values from -0.109375 to 0.109375
- w_key: bfloat16 [8, 3072, 256], P('section', 'fsdp'), may hold values from -0.109375 to 0.109375
- w_value: bfloat16 [8, 3072, 256], P('section', 'fsdp'), may hold values from -0.109375 to 0.109375
- w_out: bfloat16 [8, 256, 3072], P('section', None, 'fsdp'), may hold values from -0.375 to 0.375
Outputs:
- next_first: bfloat16 [8, 3584, 3072], P('section', 'fsdp')
- next_second: bfloat16 [8, 3584, 3072], P('section', 'fsdp')
- back_first: bfloat16 [8, 3584, 3072], P('section', 'fsdp')
- back_second: bfloat16 [8, 3584, 3072], P('section', 'fsdp')
- back_grad_first: bfloat16 [8, 3584, 3072], P('section', 'fsdp')
- back_grad_second: bfloat16 [8, 3584, 3072], P('section', 'fsdp')
- query_weight_grad: float32 [8, 3072, 256], P('section', 'fsdp')
- key_weight_grad: float32 [8, 3072, 256], P('section', 'fsdp')
- value_weight_grad: float32 [8, 3072, 256], P('section', 'fsdp')
- out_weight_grad: float32 [8, 256, 3072], P('section', None, 'fsdp')
All inputs are finite; a program needn't handle non-finite values.
Results may differ from a plain program's by a relative error of at most 0.035.
Values may be sent and summed in bfloat16 or wider, within the bound.
No kernel may reach another device: no remote copies, remote signals or barrier semaphores. Data moves between devices by JAX's collectives and lax.ppermute only.
A program may use at most 128 MiB of HBM per device.

v0:
```python
import math

import jax
import jax.numpy as jnp
from jax import lax
from jax.sharding import PartitionSpec as P

HEADS = 2
HEAD_DIM = 128


epsilon = 1e-05


def passed_along(value, axis, steps):
    count = lax.axis_size(axis)
    first, last = (max(0, -steps), min(count, count - steps))
    return lax.ppermute(value, axis, [(source, source + steps) for source in range(first, last)])


def normalize(inputs):
    widened = inputs.astype(jnp.float32)
    inverse_rms = lax.rsqrt(jnp.mean(widened * widened, axis=-1, keepdims=True) + epsilon)
    return (widened * inverse_rms, inverse_rms)


def split_heads(matrix):
    return matrix.reshape(matrix.shape[0], HEADS, HEAD_DIM)


def merge_heads(tensor):
    return tensor.reshape(tensor.shape[0], HEADS * HEAD_DIM)


def project(inputs, full_query, full_key, full_value):
    normed, inverse_rms = normalize(inputs)
    normed_half = normed.astype(jnp.bfloat16)
    queries = jnp.dot(normed_half, full_query, preferred_element_type=jnp.float32).astype(
        jnp.bfloat16
    )
    keys_own = jnp.dot(normed_half, full_key, preferred_element_type=jnp.float32).astype(
        jnp.bfloat16
    )
    values_own = jnp.dot(normed_half, full_value, preferred_element_type=jnp.float32).astype(
        jnp.bfloat16
    )
    return (normed, inverse_rms, normed_half, queries, keys_own, values_own)


def gather_pairs(keys_own, values_own):
    return (
        lax.all_gather(keys_own, "fsdp", axis=0, tiled=True),
        lax.all_gather(values_own, "fsdp", axis=0, tiled=True),
    )


def attend(queries, keys_full, values_full, query_start):
    row_count = queries.shape[0]
    key_count = keys_full.shape[0]
    scores = jnp.einsum(
        "qhd,khd->hqk",
        split_heads(queries),
        split_heads(keys_full),
        preferred_element_type=jnp.float32,
    ) / math.sqrt(HEAD_DIM)
    query_index = query_start + jnp.arange(row_count, dtype=jnp.int32)
    key_index = jnp.arange(key_count, dtype=jnp.int32)
    causal_mask = key_index[None, :] <= query_index[:, None]
    masked = jnp.where(causal_mask[None], scores, -1e30)
    highest = jnp.max(masked, axis=-1, keepdims=True)
    weights_exp = jnp.where(causal_mask[None], jnp.exp(masked - highest), 0.0)
    row_total = jnp.sum(weights_exp, axis=-1, keepdims=True)
    probs = weights_exp / row_total
    probs_half = probs.astype(jnp.bfloat16)
    attended = merge_heads(
        jnp.einsum(
            "hqk,khd->qhd", probs_half, split_heads(values_full), preferred_element_type=jnp.float32
        )
    ).astype(jnp.bfloat16)
    log_total = (highest + jnp.log(row_total))[:, :, 0]
    return (probs, probs_half, attended, log_total)


def per_device(
    fwd_first,
    fwd_second,
    bwd_first,
    bwd_second,
    grad_first,
    grad_second,
    w_query,
    w_key,
    w_value,
    w_out,
):
    full_query, full_key, full_value, full_out = (
        lax.all_gather(w_query[0], "fsdp", axis=0, tiled=True),
        lax.all_gather(w_key[0], "fsdp", axis=0, tiled=True),
        lax.all_gather(w_value[0], "fsdp", axis=0, tiled=True),
        lax.all_gather(w_out[0], "fsdp", axis=1, tiled=True),
    )
    row_count = fwd_first.shape[1]
    query_start = lax.axis_index("fsdp") * row_count
    scale = 1.0 / math.sqrt(HEAD_DIM)
    pieces = project(fwd_second[0], full_query, full_key, full_value)
    keys_full, values_full = gather_pairs(pieces[4], pieces[5])
    outcome = attend(pieces[3], keys_full, values_full, query_start)
    updated = (
        fwd_first[0].astype(jnp.float32)
        + jnp.dot(outcome[2], full_out, preferred_element_type=jnp.float32)
    ).astype(jnp.bfloat16)
    forward_pair = passed_along((fwd_second[0], updated), "section", 1)
    stream_in = bwd_first[0]
    cot_out = grad_second[0]
    normed, inverse_rms, normed_half, queries, keys_own, values_own = project(
        stream_in, full_query, full_key, full_value
    )
    keys_full, values_full = gather_pairs(keys_own, values_own)
    probs, probs_half, attended, log_total = attend(queries, keys_full, values_full, query_start)
    rec_first = (
        bwd_second[0].astype(jnp.float32)
        - jnp.dot(attended, full_out, preferred_element_type=jnp.float32)
    ).astype(jnp.bfloat16)
    attended_grad = jnp.dot(cot_out, full_out.T, preferred_element_type=jnp.float32).astype(
        jnp.bfloat16
    )
    prob_grad = jnp.einsum(
        "qhd,khd->hqk",
        split_heads(attended_grad),
        split_heads(values_full),
        preferred_element_type=jnp.float32,
    )
    row_dot = jnp.sum(probs * prob_grad, axis=-1, keepdims=True)
    score_grad = (probs * (prob_grad - row_dot) * scale).astype(jnp.bfloat16)
    query_grad = merge_heads(
        jnp.einsum(
            "hqk,khd->qhd", score_grad, split_heads(keys_full), preferred_element_type=jnp.float32
        )
    ).astype(jnp.bfloat16)
    key_part = merge_heads(
        jnp.einsum(
            "hqk,qhd->khd", score_grad, split_heads(queries), preferred_element_type=jnp.float32
        )
    )
    value_part = merge_heads(
        jnp.einsum(
            "hqk,qhd->khd",
            probs_half,
            split_heads(attended_grad),
            preferred_element_type=jnp.float32,
        )
    )
    key_sum = lax.psum_scatter(
        key_part.astype(jnp.bfloat16), "fsdp", scatter_dimension=0, tiled=True
    )
    value_sum = lax.psum_scatter(
        value_part.astype(jnp.bfloat16), "fsdp", scatter_dimension=0, tiled=True
    )
    normed_grad = jnp.dot(query_grad, full_query.T, preferred_element_type=jnp.float32)
    normed_grad = normed_grad + jnp.dot(key_sum, full_key.T, preferred_element_type=jnp.float32)
    normed_grad = normed_grad + jnp.dot(value_sum, full_value.T, preferred_element_type=jnp.float32)
    input_grad = inverse_rms * (
        normed_grad - normed * jnp.mean(normed_grad * normed, axis=-1, keepdims=True)
    )
    cot_second = (grad_first[0].astype(jnp.float32) + input_grad).astype(jnp.bfloat16)
    query_wpart = jnp.einsum(
        "td,te->de", normed_half, query_grad, preferred_element_type=jnp.float32
    )
    key_wpart = jnp.einsum("td,te->de", normed_half, key_sum, preferred_element_type=jnp.float32)
    value_wpart = jnp.einsum(
        "td,te->de", normed_half, value_sum, preferred_element_type=jnp.float32
    )
    out_wpart = jnp.einsum("te,td->ed", attended, cot_out, preferred_element_type=jnp.float32)
    weight_sums = (
        lax.psum_scatter(
            query_wpart.astype(jnp.bfloat16), "fsdp", scatter_dimension=0, tiled=True
        ).astype(jnp.float32),
        lax.psum_scatter(
            key_wpart.astype(jnp.bfloat16), "fsdp", scatter_dimension=0, tiled=True
        ).astype(jnp.float32),
        lax.psum_scatter(
            value_wpart.astype(jnp.bfloat16), "fsdp", scatter_dimension=0, tiled=True
        ).astype(jnp.float32),
        lax.psum_scatter(
            out_wpart.astype(jnp.bfloat16), "fsdp", scatter_dimension=1, tiled=True
        ).astype(jnp.float32),
    )
    moved = passed_along((rec_first, stream_in, cot_out, cot_second), "section", -1)
    backward_items = (moved, weight_sums)
    moved, weight_sums = backward_items
    return (
        forward_pair[0][None],
        forward_pair[1][None],
        moved[0][None],
        moved[1][None],
        moved[2][None],
        moved[3][None],
        weight_sums[0][None],
        weight_sums[1][None],
        weight_sums[2][None],
        weight_sums[3][None],
    )


def solution(mesh):
    placed = (
        P("section", "fsdp", None),
        P("section", "fsdp", None),
        P("section", "fsdp", None),
        P("section", "fsdp", None),
        P("section", "fsdp", None),
        P("section", "fsdp", None),
        P("section", "fsdp", None),
        P("section", "fsdp", None),
        P("section", "fsdp", None),
        P("section", None, "fsdp"),
    )
    return jax.shard_map(
        per_device,
        mesh=mesh,
        in_specs=placed,
        out_specs=(
            P("section", "fsdp", None),
            P("section", "fsdp", None),
            P("section", "fsdp", None),
            P("section", "fsdp", None),
            P("section", "fsdp", None),
            P("section", "fsdp", None),
            P("section", "fsdp", None),
            P("section", "fsdp", None),
            P("section", "fsdp", None),
            P("section", None, "fsdp"),
        ),
        check_vma=False,
    )
```

profile of v0, /device:TPU:19, one launch (start us, length us, event | category | flops | bytes accessed | tf_op | source)
XLA Modules:
  0.0 1306.6 jit_solution(2452371001347587751)
XLA Ops:
  7.2 0.7 all-gather.21.cloned.1.call-update
  8.0 0.7 all-gather.25.cloned.1.call-update
  8.7 0.7 all-gather.27.cloned.1.call-update
  9.5 0.5 all-gather.23.cloned.1.call-update
  10.0 1.3 fusion.70
  11.4 65.7 %all-gather.21.cloned.1.call-done = bf16[1,3072,256]{2,1,0:T(8,128)(2,1)} async-done(((bf16[1,96,256]{2,1,0:T(8,128)(2,1)}), bf16[1,3072,256]{2,1,0:T(8,128)(2,1)}) %all-gather.21.cloned.1.call-update) | async-done | bytes 1572880 | tf_op jit(solution)/shard_map/all_gather | solution.py:99
  77.1 2.7 fusion.77
  79.9 63.1 %all-gather.25.cloned.1.call-done = bf16[1,3072,256]{2,1,0:T(8,128)(2,1)} async-done(((bf16[1,96,256]{2,1,0:T(8,128)(2,1)}), bf16[1,3072,256]{2,1,0:T(8,128)(2,1)}) %all-gather.25.cloned.1.call-update) | async-done | bytes 1572880 | tf_op jit(solution)/shard_map/all_gather | solution.py:98
  143.0 2.5 fusion.89
  145.8 63.0 %all-gather.27.cloned.1.call-done = bf16[1,256,3072]{1,2,0:T(8,128)(2,1)} async-done(((bf16[1,256,96]{1,2,0:T(8,128)(2,1)}), bf16[1,256,3072]{1,2,0:T(8,128)(2,1)}) %all-gather.27.cloned.1.call-update) | async-done | bytes 1572880 | tf_op jit(solution)/shard_map/all_gather | solution.py:100
  208.8 1.8 fusion.109
  210.6 63.9 %all-gather.23.cloned.1.call-done = bf16[1,3072,256]{2,1,0:T(8,128)(2,1)} async-done(((bf16[1,96,256]{2,1,0:T(8,128)(2,1)}), bf16[1,3072,256]{2,1,0:T(8,128)(2,1)}) %all-gather.23.cloned.1.call-update) | async-done | bytes 1572880 | tf_op jit(solution)/shard_map/all_gather | solution.py:97
  274.5 1.8 fusion.112
  276.3 64.7 %all-gather.17.cloned.1.call-done = bf16[3584,256]{1,0:T(8,128)(2,1)} async-done(((bf16[112,256]{1,0:T(8,128)(2,1)}), bf16[3584,256]{1,0:T(8,128)(2,1)}) %all-gather.17.cloned.1.call-update) | async-done | bytes 1835024 | tf_op jit(solution)/shard_map/all_gather | solution.py:53
  341.1 3.8 fusion.23
  344.9 62.8 %all-gather.19.cloned.1.call-done = bf16[3584,256]{1,0:T(8,128)(2,1)} async-done(((bf16[112,256]{1,0:T(8,128)(2,1)}), bf16[3584,256]{1,0:T(8,128)(2,1)}) %all-gather.19.cloned.1.call-update) | async-done | bytes 1835024 | tf_op jit(solution)/shard_map/all_gather | solution.py:52
  407.6 4.9 fusion.163
  412.6 6.0 convolution_convert_fusion.1
  418.5 2.3 copy.59
  420.9 1.0 copy-done.5
  422.2 2.5 fusion.86
  424.7 1.0 fusion.74
  425.8 3.9 convolution_convert_fusion
  429.7 3.8 copy.61
  433.6 6.5 fusion.118
  440.1 1.9 convolution_convert_fusion.5
  442.0 3.2 fusion.103
  445.2 1.8 convolution_convert_fusion.2
  447.1 87.4 %reduce-scatter.19.cloned.1.call-done = bf16[112,256]{1,0:T(8,128)(2,1)} async-done(((bf16[3584,256]{1,0:T(8,128)(2,1)}), bf16[112,256]{1,0:T(8,128)(2,1)}) %reduce-scatter.19.cloned.1.call-update) | async-done | bytes 57360
  534.5 2.7 convolution_convert_fusion.4
  537.3 3.5 collective-permute-start
  540.8 3.4 collective-permute-start.3
  544.3 3.5 collective-permute-start.4
  547.8 1.8 fusion.115
  549.6 1.5 fusion.16
  551.1 4.3 collective-permute-start.2
  555.4 52.4 %all-gather.15.cloned.1.call-done = bf16[3584,256]{1,0:T(8,128)(2,1)} async-done(((bf16[112,256]{1,0:T(8,128)(2,1)}), bf16[3584,256]{1,0:T(8,128)(2,1)}) %all-gather.15.cloned.1.call-update) | async-done | bytes 1835024 | tf_op jit(solution)/shard_map/all_gather | solution.py:52
  607.7 4.9 fusion.162
  612.7 93.3 %all-gather.13.cloned.1.call-done = bf16[3584,256]{1,0:T(8,128)(2,1)} async-done(((bf16[112,256]{1,0:T(8,128)(2,1)}), bf16[3584,256]{1,0:T(8,128)(2,1)}) %all-gather.13.cloned.1.call-update) | async-done | bytes 1835024 | tf_op jit(solution)/shard_map/all_gather | solution.py:53
  706.0 3.1 fusion.106
  709.1 112.9 %reduce-scatter.21.cloned.1.call-done = bf16[112,256]{1,0:T(8,128)(2,1)} async-done(((bf16[3584,256]{1,0:T(8,128)(2,1)}), bf16[112,256]{1,0:T(8,128)(2,1)}) %reduce-scatter.21.cloned.1.call-update) | async-done | bytes 57360
  822.0 2.7 convolution_convert_fusion.3
  824.7 2.3 fusion.15
  827.0 3.5 collective-permute-start.1
  830.5 0.6 fusion.52
  831.2 0.6 convolution_add_fusion.1
  832.0 0.7 fusion.65
  833.1 0.4 fusion.69
  833.5 3.4 collective-permute-start.5
  837.0 22.4 %collective-permute-done.1 = bf16[112,3072]{1,0:T(8,128)(2,1)} collective-permute-done((bf16[112,3072]{1,0:T(8,128)(2,1)S(1)}, bf16[112,3072]{1,0:T(8,128)(2,1)}, u32[]{:S(2)}, u32[]{:S(2)}) %collective-permute-start.1) | collective-permute-done | bytes 688160 | tf_op jit(solution)/shard_map/ppermute | solution.py:18
  859.4 80.0 %reduce-scatter.11.cloned.1.call-done = bf16[96,256]{1,0:T(8,128)(2,1)} async-done(((bf16[3072,256]{1,0:T(8,128)(2,1)}), bf16[96,256]{1,0:T(8,128)(2,1)}) %reduce-scatter.11.cloned.1.call-update) | async-done | bytes 49168 | tf_op jit(solution)/shard_map/reduce_scatter | solution.py:175
  939.4 1.4 bitcast_convert_fusion.3
  940.8 114.5 %reduce-scatter.17.cloned.1.call-done = bf16[256,96]{0,1:T(8,128)(2,1)} async-done(((bf16[256,3072]{0,1:T(8,128)(2,1)}), bf16[256,96]{0,1:T(8,128)(2,1)}) %reduce-scatter.17.cloned.1.call-update) | async-done | bytes 49168 | tf_op jit(solution)/shard_map/reduce_scatter | solution.py:184
  1055.3 1.4 bitcast_convert_fusion
  1056.8 114.6 %reduce-scatter.13.cloned.1.call-done = bf16[96,256]{1,0:T(8,128)(2,1)} async-done(((bf16[3072,256]{1,0:T(8,128)(2,1)}), bf16[96,256]{1,0:T(8,128)(2,1)}) %reduce-scatter.13.cloned.1.call-update) | async-done | bytes 49168 | tf_op jit(solution)/shard_map/reduce_scatter | solution.py:178
  1171.4 1.4 bitcast_convert_fusion.2
  1172.8 115.0 %reduce-scatter.15.cloned.1.call-done = bf16[96,256]{1,0:T(8,128)(2,1)} async-done(((bf16[3072,256]{1,0:T(8,128)(2,1)}), bf16[96,256]{1,0:T(8,128)(2,1)}) %reduce-scatter.15.cloned.1.call-update) | async-done | bytes 49168 | tf_op jit(solution)/shard_map/reduce_scatter | solution.py:181
  1287.8 1.4 bitcast_convert_fusion.1
  1289.2 2.0 copy.163
  1291.2 2.0 copy.164
  1293.2 2.0 copy.165
  1295.2 2.0 copy.166
  1297.2 2.0 copy.167
  1299.2 0.8 copy.168
  (58 shorter events, 1.8 us)
Async XLA Ops:
  7.2 135.8 %copy-start = (bf16[1,112,3072]{2,1,0:T(8,128)(2,1)S(1)}, bf16[1,112,3072]{2,1,0:T(8,128)(2,1)}, u32[]{:S(2)}) copy-start(bf16[1,112,3072]{2,1,0:T(8,128)(2,1)} %param.12) | copy-start | bytes 2064388
  7.2 69.9 %all-gather.21.cloned.1.call-start = ((), (), s32[]{:S(2)}) async-start(), calls=%async_computation.14 | async-start | bytes 1622016 | tf_op jit(solution)/shard_map/all_gather | solution.py:99
  7.9 135.0 %all-gather.25.cloned.1.call-start = ((), (), s32[]{:S(2)}) async-start(), calls=%async_computation.16 | async-start | bytes 1622016 | tf_op jit(solution)/shard_map/all_gather | solution.py:98
  8.7 200.1 %all-gather.27.cloned.1.call-start = ((), (), s32[]{:S(2)}) async-start(), calls=%async_computation.17 | async-start | bytes 1622016 | tf_op jit(solution)/shard_map/all_gather | solution.py:100
  9.4 265.1 %all-gather.23.cloned.1.call-start = ((), (), s32[]{:S(2)}) async-start(), calls=%async_computation.15 | async-start | bytes 1622016 | tf_op jit(solution)/shard_map/all_gather | solution.py:97
  10.0 331.1 %all-gather.17.cloned.1.call-start = ((), (), s32[]{:S(2)}) async-start(), calls=%async_computation.8 | async-start | bytes 1892352 | tf_op jit(solution)/shard_map/all_gather | solution.py:53
  79.8 129.0 %copy-start.6 = (bf16[1,112,3072]{2,1,0:T(8,128)(2,1)S(1)}, bf16[1,112,3072]{2,1,0:T(8,128)(2,1)}, u32[]{:S(2)}) copy-start(bf16[1,112,3072]{2,1,0:T(8,128)(2,1)} %param.15) | copy-start | bytes 2064388
  79.8 327.8 %all-gather.19.cloned.1.call-start = ((), (), s32[]{:S(2)}) async-start(), calls=%async_computation.9 | async-start | bytes 1892352 | tf_op jit(solution)/shard_map/all_gather | solution.py:52
  145.4 389.1 %reduce-scatter.19.cloned.1.call-start = ((), (), s32[]{:S(2)}) async-start(), calls=%async_computation.18 | async-start | bytes 1892352
  420.8 1.1 copy-start.5
  420.8 3.8 copy-start.1
  420.9 186.9 %all-gather.15.cloned.1.call-start = ((), (), s32[]{:S(2)}) async-start(), calls=%async_computation.7 | async-start | bytes 1892352 | tf_op jit(solution)/shard_map/all_gather | solution.py:52
  424.6 281.3 %all-gather.13.cloned.1.call-start = ((), (), s32[]{:S(2)}) async-start(), calls=%async_computation.6 | async-start | bytes 1892352 | tf_op jit(solution)/shard_map/all_gather | solution.py:53
  425.8 396.2 %reduce-scatter.21.cloned.1.call-start = ((), (), s32[]{:S(2)}) async-start(), calls=%async_computation.19 | async-start | bytes 1892352
  433.6 505.8 %reduce-scatter.11.cloned.1.call-start = ((), (), s32[]{:S(2)}) async-start(), calls=%async_computation.10 | async-start | bytes 1622016 | tf_op jit(solution)/shard_map/reduce_scatter | solution.py:175
  442.0 613.3 %reduce-scatter.17.cloned.1.call-start = ((), (), s32[]{:S(2)}) async-start(), calls=%async_computation.13 | async-start | bytes 1622016 | tf_op jit(solution)/shard_map/reduce_scatter | solution.py:184
  442.0 3.2 copy-start.7
  447.0 724.3 %reduce-scatter.13.cloned.1.call-start = ((), (), s32[]{:S(2)}) async-start(), calls=%async_computation.11 | async-start | bytes 1622016 | tf_op jit(solution)/shard_map/reduce_scatter | solution.py:178
  537.3 750.5 %reduce-scatter.15.cloned.1.call-start = ((), (), s32[]{:S(2)}) async-start(), calls=%async_computation.12 | async-start | bytes 1622016 | tf_op jit(solution)/shard_map/reduce_scatter | solution.py:181
  537.3 12.3 copy-start.3
  537.3 12.3 copy-start.8
  537.3 296.2 %collective-permute-start = (bf16[112,3072]{1,0:T(8,128)(2,1)S(1)}, bf16[112,3072]{1,0:T(8,128)(2,1)}, u32[]{:S(2)}, u32[]{:S(2)}) collective-permute-start(bf16[112,3072]{1,0:T(8,128)(2,1)S(1)} %bitcast.215), channel_id=1, source_target_pairs={{0,32},{32,64},{64,96},{96,128},{128,160},{160,192},{192,224},{1,3... | collective-permute-start | bytes 2064392 | tf_op jit(solution)/shard_map/ppermute | solution.py:18
  540.8 296.1 %collective-permute-start.3 = (bf16[112,3072]{1,0:T(8,128)(2,1)S(1)}, bf16[112,3072]{1,0:T(8,128)(2,1)}, u32[]{:S(2)}, u32[]{:S(2)}) collective-permute-start(bf16[112,3072]{1,0:T(8,128)(2,1)S(1)} %bitcast.214), channel_id=1, source_target_pairs={{32,0},{64,32},{96,64},{128,96},{160,128},{192,160},{224,192},{33,... | collective-permute-start | bytes 2064392 | tf_op jit(solution)/shard_map/ppermute | solution.py:18
  544.3 292.7 %collective-permute-start.4 = (bf16[112,3072]{1,0:T(8,128)(2,1)}, bf16[112,3072]{1,0:T(8,128)(2,1)}, u32[]{:S(2)}, u32[]{:S(2)}) collective-permute-start(bf16[112,3072]{1,0:T(8,128)(2,1)} %bitcast.216), channel_id=1, source_target_pairs={{32,0},{64,32},{96,64},{128,96},{160,128},{192,160},{224,192},{33,... | collective-permute-start | bytes 2064392 | tf_op jit(solution)/shard_map/ppermute | solution.py:18
  551.1 285.9 %collective-permute-start.2 = (bf16[112,3072]{1,0:T(8,128)(2,1)}, bf16[112,3072]{1,0:T(8,128)(2,1)}, u32[]{:S(2)}, u32[]{:S(2)}) collective-permute-start(bf16[112,3072]{1,0:T(8,128)(2,1)} %fusion.16), channel_id=1, source_target_pairs={{32,0},{64,32},{96,64},{128,96},{160,128},{192,160},{224,192},{33,... | collective-permute-start | bytes 2064392 | tf_op jit(solution)/shard_map/ppermute | solution.py:18
  824.7 5.8 copy-start.4
  827.0 4.2 copy-start.2
  827.0 4.2 copy-start.10
  827.0 32.4 %collective-permute-start.1 = (bf16[112,3072]{1,0:T(8,128)(2,1)S(1)}, bf16[112,3072]{1,0:T(8,128)(2,1)}, u32[]{:S(2)}, u32[]{:S(2)}) collective-permute-start(bf16[112,3072]{1,0:T(8,128)(2,1)S(1)} %fusion.15), channel_id=1, source_target_pairs={{0,32},{32,64},{64,96},{96,128},{128,160},{160,192},{192,224},{1,3... | collective-permute-start | bytes 2064392 | tf_op jit(solution)/shard_map/ppermute | solution.py:18
  831.2 0.8 copy-start.11
  832.0 1.1 copy-start.9
  833.5 223.2 %collective-permute-start.5 = (bf16[112,3072]{1,0:T(8,128)(2,1)S(1)}, bf16[112,3072]{1,0:T(8,128)(2,1)S(1)}, u32[]{:S(2)}, u32[]{:S(2)}) collective-permute-start(bf16[112,3072]{1,0:T(8,128)(2,1)S(1)} %fusion.69), channel_id=1, source_target_pairs={{32,0},{64,32},{96,64},{128,96},{160,128},{192,160},{224,192},{33,... | collective-permute-start | bytes 2064392 | tf_op jit(solution)/shard_map/ppermute | solution.py:18
Sparse Core Ops, SparseCore 0:
  9.9 67.1 all-gather.20
  79.0 63.9 all-gather.24
  144.8 63.9 all-gather.26
  210.5 63.9 all-gather.22
  276.8 64.2 all-gather.16
  343.3 64.2 all-gather.18
  421.0 113.4 reduce-scatter.18
  537.1 70.6 all-gather.14
  610.3 95.5 all-gather.12
  708.5 113.4 reduce-scatter.20
  824.5 114.8 reduce-scatter.10
  941.9 113.3 reduce-scatter.16
  1057.8 113.5 reduce-scatter.12
  1173.9 113.8 reduce-scatter.14
where the time goes:
time: 1310 us
  waiting for transfers between devices  1180 us (90%)
  matrix products  65.2 us (5%)
  starting transfers between devices  22.2 us (2%)
  local copies, waits for them, and re-layouts  18.5 us (1%)
  between operations  14.3 us (1%)
    unnamed x16, waiting for transfers between devices  203 us
    all_gather x2, waiting for transfers between devices, gather_pairs(): lax.all_gather(values_own, 'fsdp', axis=0, tiled=True)  158 us
    all_gather x2, waiting for transfers between devices, gather_pairs(): lax.all_gather(keys_own, 'fsdp', axis=0, tiled=True)  115 us
    reduce_scatter x1, waiting for transfers between devices, per_device(): lax.psum_scatter(value_wpart.astype(jnp.bfloat16), 'fsdp', scatter_dimens...  115 us
    reduce_scatter x1, waiting for transfers between devices, per_device(): lax.psum_scatter(key_wpart.astype(jnp.bfloat16), 'fsdp', scatter_dimensio...  115 us
    reduce_scatter x1, waiting for transfers between devices, per_device(): lax.psum_scatter(out_wpart.astype(jnp.bfloat16), 'fsdp', scatter_dimensio...  114 us
    reduce_scatter x1, waiting for transfers between devices, per_device(): lax.psum_scatter(query_wpart.astype(jnp.bfloat16), 'fsdp', scatter_dimens...  80 us
    all_gather x1, waiting for transfers between devices, per_device(): lax.all_gather(w_value[0], 'fsdp', axis=0, tiled=True)  65.7 us
  transfers between devices with their start and end apart: 20, of which 15 were waited for; matrix products, arithmetic and copies ran while one was open for 5% of the time, Pallas kernels for 0%

commit v1 on v0

v1 whole, which is shorter than its diff:
```python
import math

import jax
import jax.numpy as jnp
from jax import lax
from jax.sharding import Mesh
from jax.sharding import PartitionSpec as P

HEADS = 2
HEAD_DIM = 128
Y, Z, C = 2, 8, 2
NEG = -1e30
SCALE = 1.0 / math.sqrt(HEAD_DIM)
F32 = jnp.float32
BF16 = jnp.bfloat16

epsilon = 1e-05


def passed_along(value, steps):
    count = lax.axis_size("section")
    first, last = (max(0, -steps), min(count, count - steps))
    return lax.ppermute(
        value, "section", [(source, source + steps) for source in range(first, last)]
    )


def swap(value, axis):
    return lax.ppermute(value, axis, [(0, 1), (1, 0)])


def ring(value, step):
    return lax.ppermute(value, "z", [(i, (i + step) % Z) for i in range(Z)])


def ring_gather(block):
    half = block.shape[0] // 2
    blocks = {0: block}
    ahead = behind = block
    for distance in range(1, Z // 2):
        ahead, behind = ring(ahead, -1), ring(behind, 1)
        blocks[distance], blocks[-distance] = ahead, behind
    blocks[Z // 2] = jnp.concatenate([ring(ahead[:half], -1), ring(behind[half:], 1)], axis=0)
    return blocks


def ring_reduce(parts):
    half = parts[0].shape[0] // 2
    far = parts[Z // 2].astype(BF16)
    ahead = ring(far[:half], 1).astype(F32)
    behind = ring(far[half:], -1).astype(F32)
    last = Z // 2 - 1
    ahead = jnp.concatenate([parts[last][:half] + ahead, parts[last][half:]], axis=0)
    behind = jnp.concatenate([parts[-last][:half], parts[-last][half:] + behind], axis=0)
    for distance in range(last, 0, -1):
        ahead = ring(ahead.astype(BF16), 1).astype(F32)
        behind = ring(behind.astype(BF16), -1).astype(F32)
        if distance > 1:
            ahead = ahead + parts[distance - 1]
            behind = behind + parts[1 - distance]
    return parts[0].astype(F32) + ahead + behind


def normalize(inputs):
    widened = inputs.astype(F32)
    inverse_rms = lax.rsqrt(jnp.mean(widened * widened, axis=-1, keepdims=True) + epsilon)
    return (widened * inverse_rms, inverse_rms)


def dot(left, right, left_dim=1, right_dim=0):
    return lax.dot_general(
        left, right, (((left_dim,), (right_dim,)), ((), ())), preferred_element_type=F32
    )


def chip_positions(y, z, c, tokens):
    spot = jnp.arange(tokens, dtype=jnp.int32)
    base = (y * Z + z) * (C * tokens)
    return jnp.concatenate([base + c * tokens + spot, base + (1 - c) * tokens + spot])


def placed_rows(blocks, z):
    rows, columns = blocks[0].shape[1:]
    whole = jnp.zeros((Y, Z, rows, columns), BF16)
    for distance, block in blocks.items():
        whole = lax.dynamic_update_slice(whole, block[:, None], (0, (z + distance) % Z, 0, 0))
    return whole.reshape(Y * Z * rows, columns)


def owner_parts(gradient, z):
    rows = gradient.shape[0] // (Y * Z)
    split = gradient.reshape(Y, Z, rows, gradient.shape[1])
    return {
        distance: lax.dynamic_slice(
            split, (0, (z + distance) % Z, 0, 0), (Y, 1, rows, gradient.shape[1])
        )[:, 0]
        for distance in range(1 - Z // 2, Z // 2 + 1)
    }


def attend(queries, keys, values, mask):
    scores = jnp.where(mask, dot(queries, keys, 1, 1) * SCALE, NEG)
    highest = jnp.max(scores, axis=-1, keepdims=True)
    weights = jnp.where(mask, jnp.exp(scores - highest), 0.0)
    total = jnp.sum(weights, axis=-1, keepdims=True)
    return weights, highest, total


def merged(highest, total, other_highest, other_total):
    top = jnp.maximum(highest, other_highest)
    own = jnp.exp(highest - top)
    other = jnp.exp(other_highest - top)
    whole = total * own + other_total * other
    safe = jnp.where(whole > 0.0, whole, 1.0)
    return own / safe, other / safe


def per_device(
    fwd_first,
    fwd_second,
    bwd_first,
    bwd_second,
    grad_first,
    grad_second,
    w_query,
    w_key,
    w_value,
    w_out,
):
    c, y, z = lax.axis_index("c"), lax.axis_index("yl"), lax.axis_index("z")
    tokens = fwd_first.shape[1]
    chip = C * tokens
    stream_f, stream_b, cot_out = fwd_second[0], bwd_first[0], grad_second[0]

    out_rows = w_out[0].T
    by_head = [
        jnp.concatenate(
            [
                part[:, head * HEAD_DIM : (head + 1) * HEAD_DIM]
                for part in (w_key[0], w_value[0], w_query[0], out_rows)
            ],
            axis=1,
        )
        for head in range(HEADS)
    ]
    mine = jnp.where(c == 0, by_head[0], by_head[1])
    given = jnp.where(c == 0, by_head[1], by_head[0])
    got = swap(given, "c")
    block = jnp.where(
        c == 0, jnp.concatenate([mine, got], axis=0), jnp.concatenate([got, mine], axis=0)
    )
    other_block = swap(block, "yl")
    pair = jnp.where(y == 0, jnp.stack([block, other_block]), jnp.stack([other_block, block]))
    wide = 2 * HEAD_DIM
    w_kv = placed_rows(ring_gather(pair[:, :, :wide]), z)
    w_qo = placed_rows(ring_gather(pair[:, :, wide:]), z)
    w_q, w_o = w_qo[:, :HEAD_DIM], w_qo[:, HEAD_DIM:]

    next_first = passed_along(stream_f, 1)
    back_second = passed_along(stream_b, -1)
    back_grad_first = passed_along(cot_out, -1)

    both_b = jnp.concatenate([stream_b, swap(stream_b, "c")], axis=0)
    both_f = jnp.concatenate([stream_f, swap(stream_f, "c")], axis=0)
    both_g = jnp.concatenate([cot_out, swap(cot_out, "c")], axis=0)
    normed_b, inverse_rms = normalize(both_b)
    normed_own, inverse_own = normed_b[:tokens], inverse_rms[:tokens]
    half_b = normed_b.astype(BF16)
    half_f = normalize(both_f)[0].astype(BF16)

    kv_b = dot(half_b, w_kv).astype(BF16)
    q_b = dot(half_b, w_q).astype(BF16)
    da_b = dot(both_g, w_o).astype(BF16)
    kv_f = dot(half_f, w_kv).astype(BF16)
    q_f = dot(half_f, w_q).astype(BF16)

    w_kv_other, w_qo_other = swap(w_kv, "c"), swap(w_qo, "c")
    w_q_other, w_o_other = w_qo_other[:, :HEAD_DIM], w_qo_other[:, HEAD_DIM:]

    def lend(value):
        return lax.ppermute(value, "yl", [(1, 0)])

    def give_back(value):
        return lax.ppermute(value, "yl", [(0, 1)])

    order = [0] + [d for k in range(1, Z // 2) for d in (k, -k)] + [Z // 2]
    key_index = jnp.concatenate([chip_positions(y, (z + d) % Z, c, tokens) for d in order])
    query_index = jnp.concatenate(
        [chip_positions(y, z, c, tokens), chip_positions(1 - y, z, c, tokens)]
    )
    mask = key_index[None, :] <= query_index[:, None]

    lent_b = lend(jnp.concatenate([q_b, da_b], axis=1))
    queries_b = jnp.concatenate([q_b, lent_b[:, :HEAD_DIM]], axis=0)
    grads_b = jnp.concatenate([da_b, lent_b[:, HEAD_DIM:]], axis=0)
    blocks = ring_gather(kv_b)
    kv = jnp.concatenate([blocks[d] for d in order], axis=0)
    keys_b, values_b = kv[:, :HEAD_DIM], kv[:, HEAD_DIM:]

    lent_f = lend(q_f)
    queries_f = jnp.concatenate([q_f, lent_f], axis=0)
    blocks = ring_gather(kv_f)
    kv = jnp.concatenate([blocks[d] for d in order], axis=0)
    keys_f, values_f = kv[:, :HEAD_DIM], kv[:, HEAD_DIM:]

    def exchanged(columns):
        stats = jnp.concatenate(columns, axis=1)
        sent = jnp.where(y == 0, stats[chip:], stats[:chip])
        received = swap(sent, "yl")
        none = jnp.concatenate(
            [jnp.full((chip, 1), NEG, F32), jnp.zeros((chip, len(columns) - 1), F32)], axis=1
        )
        full = jnp.where(
            y == 0,
            jnp.concatenate([none, received], axis=0),
            jnp.concatenate([received, none], axis=0),
        )
        return [full[:, k : k + 1] for k in range(len(columns))]

    def finish(weights, values, own_scale):
        partial = dot(weights.astype(BF16), values) * own_scale
        return partial[:chip] + give_back(partial[chip:].astype(BF16)).astype(F32)

    weights, highest, total = attend(queries_b, keys_b, mask=mask, values=values_b)
    prob_grad = dot(grads_b, values_b, 1, 1)
    row_part = jnp.sum(weights * prob_grad, axis=-1, keepdims=True)
    other_highest, other_total, other_row = exchanged([highest, total, row_part])
    own_scale, other_scale = merged(highest, total, other_highest, other_total)
    row_dot = row_part * own_scale + other_row * other_scale
    probs = weights * own_scale
    score_grad = (probs * (prob_grad - row_dot) * SCALE).astype(BF16)
    probs_half = probs.astype(BF16)
    kv_part = jnp.concatenate(
        [dot(score_grad, queries_b, 0, 0), dot(probs_half, grads_b, 0, 0)], axis=1
    )
    kv_grad = ring_reduce(
        {d: kv_part[i * chip : (i + 1) * chip] for i, d in enumerate(order)}
    ).astype(BF16)
    q_part = dot(score_grad, keys_b)
    q_grad = (q_part[:chip] + give_back(q_part[chip:].astype(BF16)).astype(F32)).astype(BF16)
    attended_part = dot(probs_half, values_b)
    attended_b = (
        attended_part[:chip] + give_back(attended_part[chip:].astype(BF16)).astype(F32)
    ).astype(BF16)
    attended_other = swap(attended_b[tokens:], "c")
    rec_first = (
        bwd_second[0].astype(F32)
        - dot(attended_b[:tokens], w_o, 1, 1)
        - dot(attended_other, w_o_other, 1, 1)
    ).astype(BF16)
    back_first = passed_along(rec_first, -1)

    weights, highest, total = attend(queries_f, keys_f, mask=mask, values=values_f)
    other_highest, other_total = exchanged([highest, total])
    own_scale, _ = merged(highest, total, other_highest, other_total)
    attended_f = finish(weights, values_f, own_scale).astype(BF16)
    attended_other = swap(attended_f[tokens:], "c")
    updated = (
        fwd_first[0].astype(F32)
        + dot(attended_f[:tokens], w_o, 1, 1)
        + dot(attended_other, w_o_other, 1, 1)
    ).astype(BF16)
    next_second = passed_along(updated, 1)

    grads = jnp.concatenate([kv_grad, q_grad], axis=1)
    grads_other = swap(grads[tokens:], "c")
    normed_grad = (
        dot(grads[:tokens, :wide], w_kv, 1, 1)
        + dot(grads[:tokens, wide:], w_q, 1, 1)
        + dot(grads_other[:, :wide], w_kv_other, 1, 1)
        + dot(grads_other[:, wide:], w_q_other, 1, 1)
    )
    input_grad = inverse_own * (
        normed_grad - normed_own * jnp.mean(normed_grad * normed_own, axis=-1, keepdims=True)
    )
    cot_second = (grad_first[0].astype(F32) + input_grad).astype(BF16)
    back_grad_second = passed_along(cot_second, -1)

    qo_wpart = jnp.concatenate(
        [dot(half_b, q_grad, 0, 0), dot(both_g, attended_b, 0, 0)], axis=1
    ).astype(BF16)
    kv_wpart = dot(half_b, kv_grad, 0, 0).astype(BF16)

    def summed(part):
        over_z = ring_reduce(owner_parts(part, z))
        sent = jnp.where(y == 0, over_z[1], over_z[0]).astype(BF16)
        return jnp.where(y == 0, over_z[0], over_z[1]) + swap(sent, "yl").astype(F32)

    whole = jnp.concatenate([summed(kv_wpart), summed(qo_wpart)], axis=1)
    rows = whole.shape[0] // C
    own = jnp.where(c == 0, whole[:rows], whole[rows:])
    other = swap(jnp.where(c == 0, whole[rows:], whole[:rows]), "c")

    def heads_of(index):
        span = slice(index * HEAD_DIM, (index + 1) * HEAD_DIM)
        return jnp.where(
            c == 0,
            jnp.concatenate([own[:, span], other[:, span]], axis=1),
            jnp.concatenate([other[:, span], own[:, span]], axis=1),
        )

    return (
        next_first[None],
        next_second[None],
        back_first[None],
        back_second[None],
        back_grad_first[None],
        back_grad_second[None],
        heads_of(2)[None],
        heads_of(0)[None],
        heads_of(1)[None],
        heads_of(3).T[None],
    )


def solution(mesh):
    sections = mesh.devices.shape[0]
    split = Mesh(mesh.devices.reshape(sections, Y, Z, C), ("section", "yl", "z", "c"))
    fsdp = ("yl", "z", "c")
    rows = P("section", fsdp, None)
    columns = P("section", None, fsdp)
    return jax.shard_map(
        per_device,
        mesh=split,
        in_specs=(rows,) * 9 + (columns,),
        out_specs=(rows,) * 9 + (columns,),
        check_vma=False,
    )
```

time: 1310 us -> 380 us (0.29)
  waiting for transfers between devices: 1180 us -> 163 us
  starting transfers between devices: 22.2 us -> 148 us
  matrix products: 65.2 us -> 28.6 us
    all_gather x8 -> x0, waiting for transfers between devices: 529 us -> none  [the longest x2 158 us: gather_pairs(): lax.all_gather(values_own, 'fsdp', axis=0, tiled=True)]
    reduce_scatter x4 -> x0, waiting for transfers between devices: 424 us -> none  [the longest x1 115 us: per_device(): lax.psum_scatter(value_wpart.astype(jnp.bfloat16), 'fsdp', scatter_dimens...]
    unnamed x16 -> x0, waiting for transfers between devices: 203 us -> none
    ppermute x6 -> x82, waiting for transfers between devices: 22.4 us -> 163 us  [the longest x56 81.1 us: ring(): return lax.ppermute(value, 'z', [(i, (i + step) % Z) for i in range(Z)])]
    ppermute x6 -> x82, starting transfers between devices: 21.6 us -> 148 us  [the longest x56 66.1 us: ring(): return lax.ppermute(value, 'z', [(i, (i + step) % Z) for i in range(Z)])]
    dot_general x22 -> x24, matrix products: 55.4 us -> 28.6 us  [dot(): lax.dot_general(left, right, (((left_dim,), (right_dim,)), ((), ())), pre...]
  transfers between devices with their start and end apart: 20 -> 82, of which waited for: 15 -> 43; matrix products, arithmetic and copies ran while one was open for 5% -> 14% of each run, Pallas kernels for 0% -> 0%
where the time goes in v1:
time: 380 us; the launch traced here: 375 us
  waiting for transfers between devices  163 us (43%)
  starting transfers between devices  148 us (39%)
  matrix products  28.6 us (8%)
  local copies, waits for them, and re-layouts  21.4 us (6%)
  other arithmetic  11.5 us (3%)
    ppermute x56, waiting for transfers between devices, ring(): return lax.ppermute(value, 'z', [(i, (i + step) % Z) for i in range(Z)])  81.1 us
    ppermute x15, waiting for transfers between devices, swap(): return lax.ppermute(value, axis, [(0, 1), (1, 0)])  78.1 us
    ppermute x56, starting transfers between devices, ring(): return lax.ppermute(value, 'z', [(i, (i + step) % Z) for i in range(Z)])  66.1 us
    ppermute x15, starting transfers between devices, swap(): return lax.ppermute(value, axis, [(0, 1), (1, 0)])  50.9 us
    dot_general x24, matrix products, dot(): lax.dot_general(left, right, (((left_dim,), (right_dim,)), ((), ())), pre...  28.6 us
    ppermute x6, starting transfers between devices, passed_along(): lax.ppermute(value, 'section', [(source, source + steps) for source in ra...  20.9 us
    unnamed x66, local copies, waits for them, and re-layouts  8.86 us
    ppermute x3, starting transfers between devices, give_back(): return lax.ppermute(value, 'yl', [(0, 1)])  7.76 us
  transfers between devices with their start and end apart: 82, of which 43 were waited for; matrix products, arithmetic and copies ran while one was open for 14% of the time, Pallas kernels for 0%

profile of v1, /device:TPU:19, one launch (start us, length us, event | category | flops | bytes accessed | tf_op | source)
XLA Modules:
  0.0 375.1 jit_solution(4295199646648360381)
XLA Ops:
  1.4 2.0 collective-permute-start.49
  6.9 5.7 %collective-permute-start = (bf16[112,3072]{1,0:T(8,128)(2,1)}, bf16[112,3072]{1,0:T(8,128)(2,1)}, u32[]{:S(2)}, u32[]{:S(2)}) collective-permute-start(bf16[112,3072]{1,0:T(8,128)(2,1)} %bitcast.259), channel_id=1, source_target_pairs={{0,32},{32,64},{64,96},{96,128},{128,160},{160,192},{192,224},{1,3... | collective-permute-start | bytes 2064392 | tf_op jit(solution)/shard_map/ppermute | solution.py:23
  12.6 1.9 collective-permute-start.50
  16.4 38.3 %collective-permute-done.3 = bf16[192,512]{1,0:T(8,128)(2,1)S(1)} collective-permute-done((bf16[192,512]{1,0:T(8,128)(2,1)S(1)}, bf16[192,512]{1,0:T(8,128)(2,1)S(1)}, u32[]{:S(2)}, u32[]{:S(2)}) %collective-permute-start.3) | collective-permute-done | bytes 196640 | tf_op jit(solution)/shard_map/ppermute | solution.py:29
  54.8 5.7 %collective-permute-start.13 = (bf16[2,192,256]{2,1,0:T(8,128)(2,1)S(1)}, bf16[2,192,256]{2,1,0:T(8,128)(2,1)S(1)}, u32[]{:S(2)}, u32[]{:S(2)}) collective-permute-start(bf16[2,192,256]{2,1,0:T(8,128)(2,1)S(1)} %get-tuple-element.38), channel_id=1, source_target_pairs={{0,14},{2,0},{4,2},{6,4},{8,6},{10,8},{12,10},{14,12},{1,15},{3,1}... | collective-permute-start | bytes 589832 | tf_op jit(solution)/shard_map/ppermute | solution.py:33
  63.9 3.4 collective-permute-start.4
  68.0 1.9 collective-permute-done.4
  70.0 6.2 %collective-permute-done.14 = bf16[2,192,256]{2,1,0:T(8,128)(2,1)S(1)} collective-permute-done((bf16[2,192,256]{2,1,0:T(8,128)(2,1)S(1)}, bf16[2,192,256]{2,1,0:T(8,128)(2,1)S(1)}, u32[]{:S(2)}, u32[]{:S(2)}) %collective-permute-start.14) | collective-permute-done | bytes 196640 | tf_op jit(solution)/shard_map/ppermute | solution.py:33
  76.8 5.0 %collective-permute-done.5 = bf16[2,192,256]{2,1,0:T(8,128)(2,1)S(1)} collective-permute-done((bf16[2,192,256]{2,1,0:T(8,128)(2,1)S(1)}, bf16[2,192,256]{2,1,0:T(8,128)(2,1)S(1)}, u32[]{:S(2)}, u32[]{:S(2)}) %collective-permute-start.5) | collective-permute-done | bytes 196640 | tf_op jit(solution)/shard_map/ppermute | solution.py:33
  81.8 4.9 %collective-permute-start.35 = (bf16[112,3072]{1,0:T(8,128)(2,1)S(1)}, bf16[112,3072]{1,0:T(8,128)(2,1)S(1)}, u32[]{:S(2)}, u32[]{:S(2)}) collective-permute-start(bf16[112,3072]{1,0:T(8,128)(2,1)S(1)} %bitcast.290), channel_id=1, source_target_pairs={{0,1},{1,0},{2,3},{3,2},{4,5},{5,4},{6,7},{7,6},{8,9},{9,8},{10,11... | collective-permute-start | bytes 2064392 | tf_op jit(solution)/shard_map/ppermute | solution.py:29
  89.1 2.6 collective-permute-start.6
  91.7 1.7 collective-permute-done.15
  94.1 2.4 collective-permute-done.16
  101.2 1.9 convert_multiply_fusion
  103.5 2.7 collective-permute-start.19
  106.4 2.7 collective-permute-start.10
  113.0 2.0 constant_dynamic-update-slice_fusion.17
  116.5 2.0 constant_dynamic-update-slice_fusion.8
  118.5 2.4 collective-permute-start.21
  124.3 3.6 collective-permute-done.36
  127.9 6.6 %collective-permute-start.32 = (bf16[3072,256]{1,0:T(8,128)(2,1)S(1)}, bf16[3072,256]{1,0:T(8,128)(2,1)}, u32[]{:S(2)}, u32[]{:S(2)}) collective-permute-start(bf16[3072,256]{1,0:T(8,128)(2,1)S(1)} %bitcast.240), channel_id=1, source_target_pairs={{0,1},{1,0},{2,3},{3,2},{4,5},{5,4},{6,7},{7,6},{8,9},{9,8},{10,11... | collective-permute-start | bytes 4718600 | tf_op jit(solution)/shard_map/ppermute | solution.py:29
  136.0 11.8 %collective-permute-start.39 = (bf16[224,256]{1,0:T(8,128)(2,1)S(1)}, bf16[224,256]{1,0:T(8,128)(2,1)S(1)}, u32[]{:S(2)}, u32[]{:S(2)}) collective-permute-start(bf16[224,256]{1,0:T(8,128)(2,1)S(1)} %collective-permute-done.37), channel_id=1, source_target_pairs={{0,14},{2,0},{4,2},{6,4},{8,6},{10,8},{12,10},{14,12},{1,15},{3,1}... | collective-permute-start | bytes 344072 | tf_op jit(solution)/shard_map/ppermute | solution.py:33
  147.9 1.9 collective-permute-done.39
  149.8 3.4 collective-permute-start.23
  153.4 1.7 collective-permute-done.23
  155.0 3.1 collective-permute-start.41
  158.2 1.7 collective-permute-done.41
  159.9 3.1 collective-permute-start.25
  163.1 1.6 collective-permute-done.25
  164.7 3.1 collective-permute-start.43
  169.5 3.2 collective-permute-start.27
  173.9 3.2 collective-permute-done.28
  178.0 1.9 fusion.127
  180.0 2.1 collective-permute-start.29
  184.2 3.1 collective-permute-start.30
  192.7 2.7 collective-permute-start.55
  199.4 3.4 collective-permute-start.46
  204.3 10.8 %collective-permute-start.31 = (bf16[112,128]{1,0:T(8,128)(2,1)}, bf16[112,128]{1,0:T(8,128)(2,1)}, u32[]{:S(2)}, u32[]{:S(2)}) collective-permute-start(bf16[112,128]{1,0:T(8,128)(2,1)} %slice.445), channel_id=1, source_target_pairs={{0,1},{1,0},{2,3},{3,2},{4,5},{5,4},{6,7},{7,6},{8,9},{9,8},{10,11... | collective-permute-start | bytes 86024 | tf_op jit(solution)/shard_map/ppermute | solution.py:29
  217.7 2.1 convolution_convert_fusion.2
  222.1 3.0 collective-permute-done.76
  226.5 3.5 collective-permute-done.72
  230.0 5.0 %collective-permute-done.52 = bf16[224,256]{0,1:T(8,128)(2,1)S(1)} collective-permute-done((bf16[224,256]{0,1:T(8,128)(2,1)S(1)}, bf16[224,256]{0,1:T(8,128)(2,1)S(1)}, u32[]{:S(2)}, u32[]{:S(2)}) %collective-permute-start.52) | collective-permute-done | bytes 114720 | tf_op jit(solution)/shard_map/ppermute | solution.py:33
  235.4 4.9 %collective-permute-done.53 = bf16[224,256]{0,1:T(8,128)(2,1)S(1)} collective-permute-done((bf16[224,256]{0,1:T(8,128)(2,1)S(1)}, bf16[224,256]{0,1:T(8,128)(2,1)S(1)}, u32[]{:S(2)}, u32[]{:S(2)}) %collective-permute-start.53) | collective-permute-done | bytes 114720 | tf_op jit(solution)/shard_map/ppermute | solution.py:33
  240.5 4.1 %collective-permute-done.57 = bf16[224,256]{0,1:T(8,128)(2,1)S(1)} collective-permute-done((bf16[224,256]{0,1:T(8,128)(2,1)S(1)}, bf16[224,256]{0,1:T(8,128)(2,1)S(1)}, u32[]{:S(2)}, u32[]{:S(2)}) %collective-permute-start.57) | collective-permute-done | bytes 114720 | tf_op jit(solution)/shard_map/ppermute | solution.py:33
  244.7 2.7 collective-permute-start.58
  247.6 2.0 collective-permute-done.54
  251.2 2.2 convolution_add_fusion.1
  254.7 2.4 collective-permute-done.74
  257.5 1.9 collective-permute-done.63
  261.5 3.5 collective-permute-done.78
  265.1 6.7 %collective-permute-done.64 = bf16[2,192,256]{2,1,0:T(8,128)(2,1)S(1)} collective-permute-done((bf16[2,192,256]{2,1,0:T(8,128)(2,1)S(1)}, bf16[2,192,256]{2,1,0:T(8,128)(2,1)S(1)}, u32[]{:S(2)}, u32[]{:S(2)}) %collective-permute-start.64) | collective-permute-done | bytes 196640 | tf_op jit(solution)/shard_map/ppermute | solution.py:33
  272.2 6.7 %collective-permute-done.79 = bf16[2,192,256]{2,1,0:T(8,128)(2,1)S(1)} collective-permute-done((bf16[2,192,256]{2,1,0:T(8,128)(2,1)S(1)}, bf16[2,192,256]{2,1,0:T(8,128)(2,1)S(1)}, u32[]{:S(2)}, u32[]{:S(2)}) %collective-permute-start.79) | collective-permute-done | bytes 196640 | tf_op jit(solution)/shard_map/ppermute | solution.py:33
  278.9 1.8 collective-permute-done.68
  280.7 14.6 %collective-permute-start.47 = (bf16[112,128]{1,0:T(8,128)(2,1)S(1)}, bf16[112,128]{1,0:T(8,128)(2,1)S(1)}, u32[]{:S(2)}, u32[]{:S(2)}) collective-permute-start(bf16[112,128]{1,0:T(8,128)(2,1)S(1)} %slice.460), channel_id=1, source_target_pairs={{0,1},{1,0},{2,3},{3,2},{4,5},{5,4},{6,7},{7,6},{8,9},{9,8},{10,11... | collective-permute-start | bytes 86024 | tf_op jit(solution)/shard_map/ppermute | solution.py:29
  295.5 3.6 collective-permute-done.80
  299.1 5.6 %collective-permute-start.60 = (bf16[112,384]{0,1:T(8,128)(2,1)S(1)}, bf16[112,384]{0,1:T(8,128)(2,1)S(1)}, u32[]{:S(2)}, u32[]{:S(2)}) collective-permute-start(bf16[112,384]{0,1:T(8,128)(2,1)S(1)} %pad_maximum_fusion.16), channel_id=1, source_target_pairs={{0,1},{1,0},{2,3},{3,2},{4,5},{5,4},{6,7},{7,6},{8,9},{9,8},{10,11... | collective-permute-start | bytes 258056 | tf_op jit(solution)/shard_map/ppermute | solution.py:29
  308.7 2.3 multiply_reduce_fusion.1
  311.4 4.2 %collective-permute-start.62 = (bf16[112,3072]{1,0:T(8,128)(2,1)S(1)}, bf16[112,3072]{1,0:T(8,128)(2,1)S(1)}, u32[]{:S(2)}, u32[]{:S(2)}) collective-permute-start(bf16[112,3072]{1,0:T(8,128)(2,1)S(1)} %fusion.11), channel_id=1, source_target_pairs={{32,0},{64,32},{96,64},{128,96},{160,128},{192,160},{224,192},{33,... | collective-permute-start | bytes 2064392 | tf_op jit(solution)/shard_map/ppermute | solution.py:23
  318.5 1.9 collective-permute-start.48
  324.3 5.2 %collective-permute-start.33 = (bf16[112,3072]{1,0:T(8,128)(2,1)S(1)}, bf16[112,3072]{1,0:T(8,128)(2,1)S(1)}, u32[]{:S(2)}, u32[]{:S(2)}) collective-permute-start(bf16[112,3072]{1,0:T(8,128)(2,1)S(1)} %fusion.1), channel_id=1, source_target_pairs={{0,32},{32,64},{64,96},{96,128},{128,160},{160,192},{192,224},{1,3... | collective-permute-start | bytes 2064392 | tf_op jit(solution)/shard_map/ppermute | solution.py:23
  329.4 33.0 %collective-permute-done.71 = bf16[192,256]{1,0:T(8,128)(2,1)S(1)} collective-permute-done((bf16[192,256]{1,0:T(8,128)(2,1)S(1)}, bf16[192,256]{1,0:T(8,128)(2,1)S(1)}, u32[]{:S(2)}, u32[]{:S(2)}) %collective-permute-start.71) | collective-permute-done | bytes 98336 | tf_op jit(solution)/shard_map/ppermute | solution.py:29
  362.5 1.8 collective-permute-start.81
  367.4 2.0 copy.134
  372.0 2.0 copy.138
  (317 shorter events, 76.6 us)
Async XLA Ops:
  0.6 86.1 %collective-permute-start.34 = (bf16[112,3072]{1,0:T(8,128)(2,1)}, bf16[112,3072]{1,0:T(8,128)(2,1)S(1)}, u32[]{:S(2)}, u32[]{:S(2)}) collective-permute-start(bf16[112,3072]{1,0:T(8,128)(2,1)} %bitcast.244), channel_id=1, source_target_pairs={{0,1},{1,0},{2,3},{3,2},{4,5},{5,4},{6,7},{7,6},{8,9},{9,8},{10,11... | collective-permute-start | bytes 2064392 | tf_op jit(solution)/shard_map/ppermute | solution.py:29
  1.4 87.2 %collective-permute-start.49 = (bf16[112,3072]{1,0:T(8,128)(2,1)}, bf16[112,3072]{1,0:T(8,128)(2,1)S(1)}, u32[]{:S(2)}, u32[]{:S(2)}) collective-permute-start(bf16[112,3072]{1,0:T(8,128)(2,1)} %bitcast.245), channel_id=1, source_target_pairs={{32,0},{64,32},{96,64},{128,96},{160,128},{192,160},{224,192},{33,... | collective-permute-start | bytes 2064392 | tf_op jit(solution)/shard_map/ppermute | solution.py:23
  6.5 8.7 %collective-permute-start.2 = (bf16[96,512]{1,0:T(8,128)(2,1)S(1)}, bf16[96,512]{1,0:T(8,128)(2,1)S(1)}, u32[]{:S(2)}, u32[]{:S(2)}) collective-permute-start(bf16[96,512]{1,0:T(8,128)(2,1)S(1)} %get-tuple-element.51), channel_id=1, source_target_pairs={{0,1},{1,0},{2,3},{3,2},{4,5},{5,4},{6,7},{7,6},{8,9},{9,8},{10,11... | collective-permute-start | bytes 294920 | tf_op jit(solution)/shard_map/ppermute | solution.py:29
  6.9 82.1 %collective-permute-start = (bf16[112,3072]{1,0:T(8,128)(2,1)}, bf16[112,3072]{1,0:T(8,128)(2,1)}, u32[]{:S(2)}, u32[]{:S(2)}) collective-permute-start(bf16[112,3072]{1,0:T(8,128)(2,1)} %bitcast.259), channel_id=1, source_target_pairs={{0,32},{32,64},{64,96},{96,128},{128,160},{160,192},{192,224},{1,3... | collective-permute-start | bytes 2064392 | tf_op jit(solution)/shard_map/ppermute | solution.py:23
  12.6 76.5 %collective-permute-start.50 = (bf16[112,3072]{1,0:T(8,128)(2,1)}, bf16[112,3072]{1,0:T(8,128)(2,1)}, u32[]{:S(2)}, u32[]{:S(2)}) collective-permute-start(bf16[112,3072]{1,0:T(8,128)(2,1)} %bitcast.289), channel_id=1, source_target_pairs={{32,0},{64,32},{96,64},{128,96},{160,128},{192,160},{224,192},{33,... | collective-permute-start | bytes 2064392 | tf_op jit(solution)/shard_map/ppermute | solution.py:23
  15.2 39.6 %collective-permute-start.3 = (bf16[192,512]{1,0:T(8,128)(2,1)S(1)}, bf16[192,512]{1,0:T(8,128)(2,1)S(1)}, u32[]{:S(2)}, u32[]{:S(2)}) collective-permute-start(bf16[192,512]{1,0:T(8,128)(2,1)S(1)} %maximum_select_fusion.2), channel_id=1, source_target_pairs={{0,16},{16,0},{1,17},{17,1},{2,18},{18,2},{3,19},{19,3},{4,20},{20... | collective-permute-start | bytes 589832 | tf_op jit(solution)/shard_map/ppermute | solution.py:29
  54.8 9.1 %collective-permute-start.13 = (bf16[2,192,256]{2,1,0:T(8,128)(2,1)S(1)}, bf16[2,192,256]{2,1,0:T(8,128)(2,1)S(1)}, u32[]{:S(2)}, u32[]{:S(2)}) collective-permute-start(bf16[2,192,256]{2,1,0:T(8,128)(2,1)S(1)} %get-tuple-element.38), channel_id=1, source_target_pairs={{0,14},{2,0},{4,2},{6,4},{8,6},{10,8},{12,10},{14,12},{1,15},{3,1}... | collective-permute-start | bytes 589832 | tf_op jit(solution)/shard_map/ppermute | solution.py:33
  63.9 6.0 %collective-permute-start.4 = (bf16[2,192,256]{2,1,0:T(8,128)(2,1)S(1)}, bf16[2,192,256]{2,1,0:T(8,128)(2,1)S(1)}, u32[]{:S(2)}, u32[]{:S(2)}) collective-permute-start(bf16[2,192,256]{2,1,0:T(8,128)(2,1)S(1)} %get-tuple-element.39), channel_id=1, source_target_pairs={{0,14},{2,0},{4,2},{6,4},{8,6},{10,8},{12,10},{14,12},{1,15},{3,1}... | collective-permute-start | bytes 589832 | tf_op jit(solution)/shard_map/ppermute | solution.py:33
  69.9 6.2 %collective-permute-start.14 = (bf16[2,192,256]{2,1,0:T(8,128)(2,1)S(1)}, bf16[2,192,256]{2,1,0:T(8,128)(2,1)S(1)}, u32[]{:S(2)}, u32[]{:S(2)}) collective-permute-start(bf16[2,192,256]{2,1,0:T(8,128)(2,1)S(1)} %get-tuple-element.38), channel_id=1, source_target_pairs={{0,2},{2,4},{4,6},{6,8},{8,10},{10,12},{12,14},{14,0},{1,3},{3,5},... | collective-permute-start | bytes 589832 | tf_op jit(solution)/shard_map/ppermute | solution.py:33
  76.1 5.7 %collective-permute-start.5 = (bf16[2,192,256]{2,1,0:T(8,128)(2,1)S(1)}, bf16[2,192,256]{2,1,0:T(8,128)(2,1)S(1)}, u32[]{:S(2)}, u32[]{:S(2)}) collective-permute-start(bf16[2,192,256]{2,1,0:T(8,128)(2,1)S(1)} %get-tuple-element.39), channel_id=1, source_target_pairs={{0,2},{2,4},{4,6},{6,8},{8,10},{10,12},{12,14},{14,0},{1,3},{3,5},... | collective-permute-start | bytes 589832 | tf_op jit(solution)/shard_map/ppermute | solution.py:33
  81.8 39.7 %collective-permute-start.35 = (bf16[112,3072]{1,0:T(8,128)(2,1)S(1)}, bf16[112,3072]{1,0:T(8,128)(2,1)S(1)}, u32[]{:S(2)}, u32[]{:S(2)}) collective-permute-start(bf16[112,3072]{1,0:T(8,128)(2,1)S(1)} %bitcast.290), channel_id=1, source_target_pairs={{0,1},{1,0},{2,3},{3,2},{4,5},{5,4},{6,7},{7,6},{8,9},{9,8},{10,11... | collective-permute-start | bytes 2064392 | tf_op jit(solution)/shard_map/ppermute | solution.py:29
  86.7 6.6 %collective-permute-start.15 = (bf16[2,192,256]{2,1,0:T(8,128)(2,1)S(1)}, bf16[2,192,256]{2,1,0:T(8,128)(2,1)S(1)}, u32[]{:S(2)}, u32[]{:S(2)}) collective-permute-start(bf16[2,192,256]{2,1,0:T(8,128)(2,1)S(1)} %collective-permute-done.13), channel_id=1, source_target_pairs={{0,14},{2,0},{4,2},{6,4},{8,6},{10,8},{12,10},{14,12},{1,15},{3,1}... | collective-permute-start | bytes 589832 | tf_op jit(solution)/shard_map/ppermute | solution.py:33
  88.6 14.5 %collective-permute-start.1 = (bf16[112,3072]{1,0:T(8,128)(2,1)S(1)}, bf16[112,3072]{1,0:T(8,128)(2,1)S(1)}, u32[]{:S(2)}, u32[]{:S(2)}) collective-permute-start(bf16[112,3072]{1,0:T(8,128)(2,1)S(1)} %bitcast.260), channel_id=1, source_target_pairs={{0,1},{1,0},{2,3},{3,2},{4,5},{5,4},{6,7},{7,6},{8,9},{9,8},{10,11... | collective-permute-start | bytes 2064392 | tf_op jit(solution)/shard_map/ppermute | solution.py:29
  89.0 7.5 %collective-permute-start.16 = (bf16[2,192,256]{2,1,0:T(8,128)(2,1)S(1)}, bf16[2,192,256]{2,1,0:T(8,128)(2,1)S(1)}, u32[]{:S(2)}, u32[]{:S(2)}) collective-permute-start(bf16[2,192,256]{2,1,0:T(8,128)(2,1)S(1)} %collective-permute-done.14), channel_id=1, source_target_pairs={{0,2},{2,4},{4,6},{6,8},{8,10},{10,12},{12,14},{14,0},{1,3},{3,5},... | collective-permute-start | bytes 589832 | tf_op jit(solution)/shard_map/ppermute | solution.py:33
  89.1 8.5 %collective-permute-start.6 = (bf16[2,192,256]{2,1,0:T(8,128)(2,1)S(1)}, bf16[2,192,256]{2,1,0:T(8,128)(2,1)S(1)}, u32[]{:S(2)}, u32[]{:S(2)}) collective-permute-start(bf16[2,192,256]{2,1,0:T(8,128)(2,1)S(1)} %collective-permute-done.4), channel_id=1, source_target_pairs={{0,14},{2,0},{4,2},{6,4},{8,6},{10,8},{12,10},{14,12},{1,15},{3,1}... | collective-permute-start | bytes 589832 | tf_op jit(solution)/shard_map/ppermute | solution.py:33
  93.4 6.4 %collective-permute-start.7 = (bf16[2,192,256]{2,1,0:T(8,128)(2,1)S(1)}, bf16[2,192,256]{2,1,0:T(8,128)(2,1)S(1)}, u32[]{:S(2)}, u32[]{:S(2)}) collective-permute-start(bf16[2,192,256]{2,1,0:T(8,128)(2,1)S(1)} %collective-permute-done.5), channel_id=1, source_target_pairs={{0,2},{2,4},{4,6},{6,8},{8,10},{10,12},{12,14},{14,0},{1,3},{3,5},... | collective-permute-start | bytes 589832 | tf_op jit(solution)/shard_map/ppermute | solution.py:33
  96.5 7.0 %collective-permute-start.17 = (bf16[2,192,256]{2,1,0:T(8,128)(2,1)S(1)}, bf16[2,192,256]{2,1,0:T(8,128)(2,1)S(1)}, u32[]{:S(2)}, u32[]{:S(2)}) collective-permute-start(bf16[2,192,256]{2,1,0:T(8,128)(2,1)S(1)} %collective-permute-done.15), channel_id=1, source_target_pairs={{0,14},{2,0},{4,2},{6,4},{8,6},{10,8},{12,10},{14,12},{1,15},{3,1}... | collective-permute-start | bytes 589832 | tf_op jit(solution)/shard_map/ppermute | solution.py:33
  97.6 8.7 %collective-permute-start.18 = (bf16[2,192,256]{2,1,0:T(8,128)(2,1)S(1)}, bf16[2,192,256]{2,1,0:T(8,128)(2,1)S(1)}, u32[]{:S(2)}, u32[]{:S(2)}) collective-permute-start(bf16[2,192,256]{2,1,0:T(8,128)(2,1)S(1)} %collective-permute-done.16), channel_id=1, source_target_pairs={{0,2},{2,4},{4,6},{6,8},{8,10},{10,12},{12,14},{14,0},{1,3},{3,5},... | collective-permute-start | bytes 589832 | tf_op jit(solution)/shard_map/ppermute | solution.py:33
  99.8 6.5 %collective-permute-start.8 = (bf16[2,192,256]{2,1,0:T(8,128)(2,1)S(1)}, bf16[2,192,256]{2,1,0:T(8,128)(2,1)S(1)}, u32[]{:S(2)}, u32[]{:S(2)}) collective-permute-start(bf16[2,192,256]{2,1,0:T(8,128)(2,1)S(1)} %collective-permute-done.6), channel_id=1, source_target_pairs={{0,14},{2,0},{4,2},{6,4},{8,6},{10,8},{12,10},{14,12},{1,15},{3,1}... | collective-permute-start | bytes 589832 | tf_op jit(solution)/shard_map/ppermute | solution.py:33
  103.1 6.0 %collective-permute-start.9 = (bf16[2,192,256]{2,1,0:T(8,128)(2,1)S(1)}, bf16[2,192,256]{2,1,0:T(8,128)(2,1)S(1)}, u32[]{:S(2)}, u32[]{:S(2)}) collective-permute-start(bf16[2,192,256]{2,1,0:T(8,128)(2,1)S(1)} %collective-permute-done.7), channel_id=1, source_target_pairs={{0,2},{2,4},{4,6},{6,8},{8,10},{10,12},{12,14},{14,0},{1,3},{3,5},... | collective-permute-start | bytes 589832 | tf_op jit(solution)/shard_map/ppermute | solution.py:33
  103.5 7.1 %collective-permute-start.19 = (bf16[1,192,256]{2,1,0:T(8,128)(2,1)S(1)}, bf16[1,192,256]{2,1,0:T(8,128)(2,1)S(1)}, u32[]{:S(2)}, u32[]{:S(2)}) collective-permute-start(bf16[1,192,256]{2,1,0:T(8,128)(2,1)S(1)} %slice.431), channel_id=1, source_target_pairs={{0,14},{2,0},{4,2},{6,4},{8,6},{10,8},{12,10},{14,12},{1,15},{3,1}... | collective-permute-start | bytes 294920 | tf_op jit(solution)/shard_map/ppermute | solution.py:33
  106.2 6.0 %collective-permute-start.20 = (bf16[1,192,256]{2,1,0:T(8,128)(2,1)S(1)}, bf16[1,192,256]{2,1,0:T(8,128)(2,1)S(1)}, u32[]{:S(2)}, u32[]{:S(2)}) collective-permute-start(bf16[1,192,256]{2,1,0:T(8,128)(2,1)S(1)} %slice.432), channel_id=1, source_target_pairs={{0,2},{2,4},{4,6},{6,8},{8,10},{10,12},{12,14},{14,0},{1,3},{3,5},... | collective-permute-start | bytes 294920 | tf_op jit(solution)/shard_map/ppermute | solution.py:33
  106.4 12.1 %collective-permute-start.10 = (bf16[1,192,256]{2,1,0:T(8,128)(2,1)S(1)}, bf16[1,192,256]{2,1,0:T(8,128)(2,1)S(1)}, u32[]{:S(2)}, u32[]{:S(2)}) collective-permute-start(bf16[1,192,256]{2,1,0:T(8,128)(2,1)S(1)} %slice.427), channel_id=1, source_target_pairs={{0,14},{2,0},{4,2},{6,4},{8,6},{10,8},{12,10},{14,12},{1,15},{3,1}... | collective-permute-start | bytes 294920 | tf_op jit(solution)/shard_map/ppermute | solution.py:33
  109.1 11.8 %collective-permute-start.11 = (bf16[1,192,256]{2,1,0:T(8,128)(2,1)S(1)}, bf16[1,192,256]{2,1,0:T(8,128)(2,1)S(1)}, u32[]{:S(2)}, u32[]{:S(2)}) collective-permute-start(bf16[1,192,256]{2,1,0:T(8,128)(2,1)S(1)} %slice.428), channel_id=1, source_target_pairs={{0,2},{2,4},{4,6},{6,8},{8,10},{10,12},{12,14},{14,0},{1,3},{3,5},... | collective-permute-start | bytes 294920 | tf_op jit(solution)/shard_map/ppermute | solution.py:33
  114.9 19.6 %collective-permute-start.37 = (bf16[224,256]{1,0:T(8,128)(2,1)S(1)}, bf16[224,256]{1,0:T(8,128)(2,1)S(1)}, u32[]{:S(2)}, u32[]{:S(2)}) collective-permute-start(bf16[224,256]{1,0:T(8,128)(2,1)S(1)} %get-tuple-element.67), channel_id=1, source_target_pairs={{0,14},{2,0},{4,2},{6,4},{8,6},{10,8},{12,10},{14,12},{1,15},{3,1}... | collective-permute-start | bytes 344072 | tf_op jit(solution)/shard_map/ppermute | solution.py:33
  116.1 18.5 %collective-permute-start.38 = (bf16[224,256]{1,0:T(8,128)(2,1)S(1)}, bf16[224,256]{1,0:T(8,128)(2,1)S(1)}, u32[]{:S(2)}, u32[]{:S(2)}) collective-permute-start(bf16[224,256]{1,0:T(8,128)(2,1)S(1)} %get-tuple-element.67), channel_id=1, source_target_pairs={{0,2},{2,4},{4,6},{6,8},{8,10},{10,12},{12,14},{14,0},{1,3},{3,5},... | collective-permute-start | bytes 344072 | tf_op jit(solution)/shard_map/ppermute | solution.py:33
  118.5 17.4 %collective-permute-start.21 = (bf16[224,256]{1,0:T(8,128)(2,1)S(1)}, bf16[224,256]{1,0:T(8,128)(2,1)S(1)}, u32[]{:S(2)}, u32[]{:S(2)}) collective-permute-start(bf16[224,256]{1,0:T(8,128)(2,1)S(1)} %get-tuple-element.63), channel_id=1, source_target_pairs={{0,14},{2,0},{4,2},{6,4},{8,6},{10,8},{12,10},{14,12},{1,15},{3,1}... | collective-permute-start | bytes 344072 | tf_op jit(solution)/shard_map/ppermute | solution.py:33
  120.9 26.9 %collective-permute-start.22 = (bf16[224,256]{1,0:T(8,128)(2,1)S(1)}, bf16[224,256]{1,0:T(8,128)(2,1)S(1)}, u32[]{:S(2)}, u32[]{:S(2)}) collective-permute-start(bf16[224,256]{1,0:T(8,128)(2,1)S(1)} %get-tuple-element.63), channel_id=1, source_target_pairs={{0,2},{2,4},{4,6},{6,8},{8,10},{10,12},{12,14},{14,0},{1,3},{3,5},... | collective-permute-start | bytes 344072 | tf_op jit(solution)/shard_map/ppermute | solution.py:33
  122.4 5.5 %collective-permute-start.36 = (bf16[224,256]{1,0:T(8,128)(2,1)S(1)}, bf16[224,256]{1,0:T(8,128)(2,1)S(1)}, u32[]{:S(2)}, u32[]{:S(2)}) collective-permute-start(bf16[224,256]{1,0:T(8,128)(2,1)S(1)} %pad_maximum_fusion.13), channel_id=1, source_target_pairs={{16,0},{17,1},{18,2},{19,3},{20,4},{21,5},{22,6},{23,7},{24,8},{25... | collective-permute-start | bytes 344072 | tf_op jit(solution)/shard_map/ppermute | solution.py:181
  127.9 177.8 %collective-permute-start.32 = (bf16[3072,256]{1,0:T(8,128)(2,1)S(1)}, bf16[3072,256]{1,0:T(8,128)(2,1)}, u32[]{:S(2)}, u32[]{:S(2)}) collective-permute-start(bf16[3072,256]{1,0:T(8,128)(2,1)S(1)} %bitcast.240), channel_id=1, source_target_pairs={{0,1},{1,0},{2,3},{3,2},{4,5},{5,4},{6,7},{7,6},{8,9},{9,8},{10,11... | collective-permute-start | bytes 4718600 | tf_op jit(solution)/shard_map/ppermute | solution.py:29
  134.5 174.2 %collective-permute-start.61 = (bf16[3072,256]{1,0:T(8,128)(2,1)}, bf16[3072,256]{1,0:T(8,128)(2,1)}, u32[]{:S(2)}, u32[]{:S(2)}) collective-permute-start(bf16[3072,256]{1,0:T(8,128)(2,1)} %bitcast.44), channel_id=1, source_target_pairs={{0,1},{1,0},{2,3},{3,2},{4,5},{5,4},{6,7},{7,6},{8,9},{9,8},{10,11... | collective-permute-start | bytes 4718600 | tf_op jit(solution)/shard_map/ppermute | solution.py:29
  134.6 42.6 %collective-permute-start.12 = (bf16[224,128]{1,0:T(8,128)(2,1)S(1)}, bf16[224,128]{1,0:T(8,128)(2,1)S(1)}, u32[]{:S(2)}, u32[]{:S(2)}) collective-permute-start(bf16[224,128]{1,0:T(8,128)(2,1)S(1)} %convolution_convert_fusion.7), channel_id=1, source_target_pairs={{16,0},{17,1},{18,2},{19,3},{20,4},{21,5},{22,6},{23,7},{24,8},{25... | collective-permute-start | bytes 172040 | tf_op jit(solution)/shard_map/ppermute | solution.py:181
  136.0 13.8 %collective-permute-start.39 = (bf16[224,256]{1,0:T(8,128)(2,1)S(1)}, bf16[224,256]{1,0:T(8,128)(2,1)S(1)}, u32[]{:S(2)}, u32[]{:S(2)}) collective-permute-start(bf16[224,256]{1,0:T(8,128)(2,1)S(1)} %collective-permute-done.37), channel_id=1, source_target_pairs={{0,14},{2,0},{4,2},{6,4},{8,6},{10,8},{12,10},{14,12},{1,15},{3,1}... | collective-permute-start | bytes 344072 | tf_op jit(solution)/shard_map/ppermute | solution.py:33
  147.8 5.4 %collective-permute-start.40 = (bf16[224,256]{1,0:T(8,128)(2,1)S(1)}, bf16[224,256]{1,0:T(8,128)(2,1)S(1)}, u32[]{:S(2)}, u32[]{:S(2)}) collective-permute-start(bf16[224,256]{1,0:T(8,128)(2,1)S(1)} %collective-permute-done.38), channel_id=1, source_target_pairs={{0,2},{2,4},{4,6},{6,8},{8,10},{10,12},{12,14},{14,0},{1,3},{3,5},... | collective-permute-start | bytes 344072 | tf_op jit(solution)/shard_map/ppermute | solution.py:33
  149.8 5.2 %collective-permute-start.23 = (bf16[224,256]{1,0:T(8,128)(2,1)S(1)}, bf16[224,256]{1,0:T(8,128)(2,1)S(1)}, u32[]{:S(2)}, u32[]{:S(2)}) collective-permute-start(bf16[224,256]{1,0:T(8,128)(2,1)S(1)} %collective-permute-done.21), channel_id=1, source_target_pairs={{0,14},{2,0},{4,2},{6,4},{8,6},{10,8},{12,10},{14,12},{1,15},{3,1}... | collective-permute-start | bytes 344072 | tf_op jit(solution)/shard_map/ppermute | solution.py:33
  167.9 5.1 %collective-permute-start.44 = (bf16[112,256]{1,0:T(8,128)(2,1)S(1)}, bf16[112,256]{1,0:T(8,128)(2,1)S(1)}, u32[]{:S(2)}, u32[]{:S(2)}) collective-permute-start(bf16[112,256]{1,0:T(8,128)(2,1)S(1)} %slice.449), channel_id=1, source_target_pairs={{0,2},{2,4},{4,6},{6,8},{8,10},{10,12},{12,14},{14,0},{1,3},{3,5},... | collective-permute-start | bytes 172040 | tf_op jit(solution)/shard_map/ppermute | solution.py:33
  182.2 5.1 %collective-permute-start.45 = (f32[224,3]{0,1:T(4,128)S(1)}, f32[224,3]{0,1:T(4,128)S(1)}, u32[]{:S(2)}, u32[]{:S(2)}) collective-permute-start(f32[224,3]{0,1:T(4,128)S(1)} %slice_select_fusion), channel_id=1, source_target_pairs={{0,16},{16,0},{1,17},{17,1},{2,18},{18,2},{3,19},{19,3},{4,20},{20... | collective-permute-start | bytes 8072 | tf_op jit(solution)/shard_map/ppermute | solution.py:29
  184.2 11.7 %collective-permute-start.30 = (bf16[224,128]{1,0:T(8,128)(2,1)S(1)}, bf16[224,128]{1,0:T(8,128)(2,1)S(1)}, u32[]{:S(2)}, u32[]{:S(2)}) collective-permute-start(bf16[224,128]{1,0:T(8,128)(2,1)S(1)} %slice.722), channel_id=1, source_target_pairs={{0,16},{1,17},{2,18},{3,19},{4,20},{5,21},{6,22},{7,23},{8,24},{9,... | collective-permute-start | bytes 172040 | tf_op jit(solution)/shard_map/ppermute | solution.py:184
  192.7 11.7 %collective-permute-start.51 = (bf16[112,256]{0,1:T(8,128)(2,1)S(1)}, bf16[112,256]{0,1:T(8,128)(2,1)S(1)}, u32[]{:S(2)}, u32[]{:S(2)}) collective-permute-start(bf16[112,256]{0,1:T(8,128)(2,1)S(1)} %get-tuple-element.32), channel_id=1, source_target_pairs={{0,2},{2,4},{4,6},{6,8},{8,10},{10,12},{12,14},{14,0},{1,3},{3,5},... | collective-permute-start | bytes 172040 | tf_op jit(solution)/shard_map/ppermute | solution.py:33
  192.7 22.5 %collective-permute-start.55 = (bf16[112,256]{0,1:T(8,128)(2,1)S(1)}, bf16[112,256]{0,1:T(8,128)(2,1)S(1)}, u32[]{:S(2)}, u32[]{:S(2)}) collective-permute-start(bf16[112,256]{0,1:T(8,128)(2,1)S(1)} %get-tuple-element.33), channel_id=1, source_target_pairs={{0,14},{2,0},{4,2},{6,4},{8,6},{10,8},{12,10},{14,12},{1,15},{3,1}... | collective-permute-start | bytes 172040 | tf_op jit(solution)/shard_map/ppermute | solution.py:33
  199.4 17.4 %collective-permute-start.46 = (bf16[224,128]{1,0:T(8,128)(2,1)}, bf16[224,128]{1,0:T(8,128)(2,1)}, u32[]{:S(2)}, u32[]{:S(2)}) collective-permute-start(bf16[224,128]{1,0:T(8,128)(2,1)} %slice.721), channel_id=1, source_target_pairs={{0,16},{1,17},{2,18},{3,19},{4,20},{5,21},{6,22},{7,23},{8,24},{9,... | collective-permute-start | bytes 172040 | tf_op jit(solution)/shard_map/ppermute | solution.py:184
  204.3 118.4 %collective-permute-start.31 = (bf16[112,128]{1,0:T(8,128)(2,1)}, bf16[112,128]{1,0:T(8,128)(2,1)}, u32[]{:S(2)}, u32[]{:S(2)}) collective-permute-start(bf16[112,128]{1,0:T(8,128)(2,1)} %slice.445), channel_id=1, source_target_pairs={{0,1},{1,0},{2,3},{3,2},{4,5},{5,4},{6,7},{7,6},{8,9},{9,8},{10,11... | collective-permute-start | bytes 86024 | tf_op jit(solution)/shard_map/ppermute | solution.py:29
  216.8 18.5 %collective-permute-start.56 = (bf16[224,256]{0,1:T(8,128)(2,1)}, bf16[224,256]{0,1:T(8,128)(2,1)S(1)}, u32[]{:S(2)}, u32[]{:S(2)}) collective-permute-start(bf16[224,256]{0,1:T(8,128)(2,1)} %pad_maximum_fusion.12), channel_id=1, source_target_pairs={{0,14},{2,0},{4,2},{6,4},{8,6},{10,8},{12,10},{14,12},{1,15},{3,1}... | collective-permute-start | bytes 344072 | tf_op jit(solution)/shard_map/ppermute | solution.py:33
  235.1 5.1 %collective-permute-start.53 = (bf16[224,256]{0,1:T(8,128)(2,1)S(1)}, bf16[224,256]{0,1:T(8,128)(2,1)S(1)}, u32[]{:S(2)}, u32[]{:S(2)}) collective-permute-start(bf16[224,256]{0,1:T(8,128)(2,1)S(1)} %fusion.51), channel_id=1, source_target_pairs={{0,2},{2,4},{4,6},{6,8},{8,10},{10,12},{12,14},{14,0},{1,3},{3,5},... | collective-permute-start | bytes 344072 | tf_op jit(solution)/shard_map/ppermute | solution.py:33
  235.3 9.5 %collective-permute-start.73 = (bf16[2,192,256]{2,1,0:T(8,128)(2,1)S(1)}, bf16[2,192,256]{2,1,0:T(8,128)(2,1)S(1)}, u32[]{:S(2)}, u32[]{:S(2)}) collective-permute-start(bf16[2,192,256]{2,1,0:T(8,128)(2,1)S(1)} %pad_maximum_fusion.9), channel_id=1, source_target_pairs={{0,2},{2,4},{4,6},{6,8},{8,10},{10,12},{12,14},{14,0},{1,3},{3,5},... | collective-permute-start | bytes 589832 | tf_op jit(solution)/shard_map/ppermute | solution.py:33
  244.6 5.0 %collective-permute-start.54 = (bf16[224,256]{0,1:T(8,128)(2,1)S(1)}, bf16[224,256]{0,1:T(8,128)(2,1)S(1)}, u32[]{:S(2)}, u32[]{:S(2)}) collective-permute-start(bf16[224,256]{0,1:T(8,128)(2,1)S(1)} %get-tuple-element.15), channel_id=1, source_target_pairs={{0,2},{2,4},{4,6},{6,8},{8,10},{10,12},{12,14},{14,0},{1,3},{3,5},... | collective-permute-start | bytes 344072 | tf_op jit(solution)/shard_map/ppermute | solution.py:33
  244.7 5.3 %collective-permute-start.58 = (bf16[224,256]{0,1:T(8,128)(2,1)S(1)}, bf16[224,256]{0,1:T(8,128)(2,1)S(1)}, u32[]{:S(2)}, u32[]{:S(2)}) collective-permute-start(bf16[224,256]{0,1:T(8,128)(2,1)S(1)} %fusion.60), channel_id=1, source_target_pairs={{0,14},{2,0},{4,2},{6,4},{8,6},{10,8},{12,10},{14,12},{1,15},{3,1}... | collective-permute-start | bytes 344072 | tf_op jit(solution)/shard_map/ppermute | solution.py:33
  249.6 5.1 %collective-permute-start.77 = (bf16[2,192,256]{2,1,0:T(8,128)(2,1)S(1)}, bf16[2,192,256]{2,1,0:T(8,128)(2,1)S(1)}, u32[]{:S(2)}, u32[]{:S(2)}) collective-permute-start(bf16[2,192,256]{2,1,0:T(8,128)(2,1)S(1)} %pad_maximum_fusion.10), channel_id=1, source_target_pairs={{0,14},{2,0},{4,2},{6,4},{8,6},{10,8},{12,10},{14,12},{1,15},{3,1}... | collective-permute-start | bytes 589832 | tf_op jit(solution)/shard_map/ppermute | solution.py:33
  250.1 7.0 %collective-permute-start.74 = (bf16[2,192,256]{2,1,0:T(8,128)(2,1)S(1)}, bf16[2,192,256]{2,1,0:T(8,128)(2,1)S(1)}, u32[]{:S(2)}, u32[]{:S(2)}) collective-permute-start(bf16[2,192,256]{2,1,0:T(8,128)(2,1)S(1)} %fusion.38), channel_id=1, source_target_pairs={{0,2},{2,4},{4,6},{6,8},{8,10},{10,12},{12,14},{14,0},{1,3},{3,5},... | collective-permute-start | bytes 589832 | tf_op jit(solution)/shard_map/ppermute | solution.py:33
  259.3 5.6 %collective-permute-start.78 = (bf16[2,192,256]{2,1,0:T(8,128)(2,1)S(1)}, bf16[2,192,256]{2,1,0:T(8,128)(2,1)S(1)}, u32[]{:S(2)}, u32[]{:S(2)}) collective-permute-start(bf16[2,192,256]{2,1,0:T(8,128)(2,1)S(1)} %get-tuple-element.28), channel_id=1, source_target_pairs={{0,14},{2,0},{4,2},{6,4},{8,6},{10,8},{12,10},{14,12},{1,15},{3,1}... | collective-permute-start | bytes 589832 | tf_op jit(solution)/shard_map/ppermute | solution.py:33
  260.6 11.5 %collective-permute-start.75 = (bf16[2,192,256]{2,1,0:T(8,128)(2,1)S(1)}, bf16[2,192,256]{2,1,0:T(8,128)(2,1)S(1)}, u32[]{:S(2)}, u32[]{:S(2)}) collective-permute-start(bf16[2,192,256]{2,1,0:T(8,128)(2,1)S(1)} %get-tuple-element.27), channel_id=1, source_target_pairs={{0,2},{2,4},{4,6},{6,8},{8,10},{10,12},{12,14},{14,0},{1,3},{3,5},... | collective-permute-start | bytes 589832 | tf_op jit(solution)/shard_map/ppermute | solution.py:33
  265.0 6.8 %collective-permute-start.64 = (bf16[2,192,256]{2,1,0:T(8,128)(2,1)S(1)}, bf16[2,192,256]{2,1,0:T(8,128)(2,1)S(1)}, u32[]{:S(2)}, u32[]{:S(2)}) collective-permute-start(bf16[2,192,256]{2,1,0:T(8,128)(2,1)S(1)} %pad_maximum_fusion.7), channel_id=1, source_target_pairs={{0,2},{2,4},{4,6},{6,8},{8,10},{10,12},{12,14},{14,0},{1,3},{3,5},... | collective-permute-start | bytes 589832 | tf_op jit(solution)/shard_map/ppermute | solution.py:33
  271.8 7.1 %collective-permute-start.79 = (bf16[2,192,256]{2,1,0:T(8,128)(2,1)S(1)}, bf16[2,192,256]{2,1,0:T(8,128)(2,1)S(1)}, u32[]{:S(2)}, u32[]{:S(2)}) collective-permute-start(bf16[2,192,256]{2,1,0:T(8,128)(2,1)S(1)} %fusion.35), channel_id=1, source_target_pairs={{0,14},{2,0},{4,2},{6,4},{8,6},{10,8},{12,10},{14,12},{1,15},{3,1}... | collective-permute-start | bytes 589832 | tf_op jit(solution)/shard_map/ppermute | solution.py:33
  272.1 8.6 %collective-permute-start.68 = (bf16[2,192,256]{2,1,0:T(8,128)(2,1)S(1)}, bf16[2,192,256]{2,1,0:T(8,128)(2,1)S(1)}, u32[]{:S(2)}, u32[]{:S(2)}) collective-permute-start(bf16[2,192,256]{2,1,0:T(8,128)(2,1)S(1)} %pad_maximum_fusion.8), channel_id=1, source_target_pairs={{0,14},{2,0},{4,2},{6,4},{8,6},{10,8},{12,10},{14,12},{1,15},{3,1}... | collective-permute-start | bytes 589832 | tf_op jit(solution)/shard_map/ppermute | solution.py:33
  278.8 16.5 %collective-permute-start.65 = (bf16[2,192,256]{2,1,0:T(8,128)(2,1)S(1)}, bf16[2,192,256]{2,1,0:T(8,128)(2,1)S(1)}, u32[]{:S(2)}, u32[]{:S(2)}) collective-permute-start(bf16[2,192,256]{2,1,0:T(8,128)(2,1)S(1)} %fusion.43), channel_id=1, source_target_pairs={{0,2},{2,4},{4,6},{6,8},{8,10},{10,12},{12,14},{14,0},{1,3},{3,5},... | collective-permute-start | bytes 589832 | tf_op jit(solution)/shard_map/ppermute | solution.py:33
  280.7 36.3 %collective-permute-start.47 = (bf16[112,128]{1,0:T(8,128)(2,1)S(1)}, bf16[112,128]{1,0:T(8,128)(2,1)S(1)}, u32[]{:S(2)}, u32[]{:S(2)}) collective-permute-start(bf16[112,128]{1,0:T(8,128)(2,1)S(1)} %slice.460), channel_id=1, source_target_pairs={{0,1},{1,0},{2,3},{3,2},{4,5},{5,4},{6,7},{7,6},{8,9},{9,8},{10,11... | collective-permute-start | bytes 86024 | tf_op jit(solution)/shard_map/ppermute | solution.py:29
  299.1 6.6 %collective-permute-start.60 = (bf16[112,384]{0,1:T(8,128)(2,1)S(1)}, bf16[112,384]{0,1:T(8,128)(2,1)S(1)}, u32[]{:S(2)}, u32[]{:S(2)}) collective-permute-start(bf16[112,384]{0,1:T(8,128)(2,1)S(1)} %pad_maximum_fusion.16), channel_id=1, source_target_pairs={{0,1},{1,0},{2,3},{3,2},{4,5},{5,4},{6,7},{7,6},{8,9},{9,8},{10,11... | collective-permute-start | bytes 258056 | tf_op jit(solution)/shard_map/ppermute | solution.py:29
  305.7 10.0 %collective-permute-start.69 = (bf16[2,192,256]{2,1,0:T(8,128)(2,1)S(1)}, bf16[2,192,256]{2,1,0:T(8,128)(2,1)S(1)}, u32[]{:S(2)}, u32[]{:S(2)}) collective-permute-start(bf16[2,192,256]{2,1,0:T(8,128)(2,1)S(1)} %get-tuple-element.20), channel_id=1, source_target_pairs={{0,14},{2,0},{4,2},{6,4},{8,6},{10,8},{12,10},{14,12},{1,15},{3,1}... | collective-permute-start | bytes 589832 | tf_op jit(solution)/shard_map/ppermute | solution.py:33
  305.7 14.8 %collective-permute-start.66 = (bf16[2,192,256]{2,1,0:T(8,128)(2,1)S(1)}, bf16[2,192,256]{2,1,0:T(8,128)(2,1)S(1)}, u32[]{:S(2)}, u32[]{:S(2)}) collective-permute-start(bf16[2,192,256]{2,1,0:T(8,128)(2,1)S(1)} %get-tuple-element.19), channel_id=1, source_target_pairs={{0,2},{2,4},{4,6},{6,8},{8,10},{10,12},{12,14},{14,0},{1,3},{3,5},... | collective-permute-start | bytes 589832 | tf_op jit(solution)/shard_map/ppermute | solution.py:33
  311.4 56.0 %collective-permute-start.62 = (bf16[112,3072]{1,0:T(8,128)(2,1)S(1)}, bf16[112,3072]{1,0:T(8,128)(2,1)S(1)}, u32[]{:S(2)}, u32[]{:S(2)}) collective-permute-start(bf16[112,3072]{1,0:T(8,128)(2,1)S(1)} %fusion.11), channel_id=1, source_target_pairs={{32,0},{64,32},{96,64},{128,96},{160,128},{192,160},{224,192},{33,... | collective-permute-start | bytes 2064392 | tf_op jit(solution)/shard_map/ppermute | solution.py:23
  315.7 5.3 %collective-permute-start.70 = (bf16[2,192,256]{2,1,0:T(8,128)(2,1)S(1)}, bf16[2,192,256]{2,1,0:T(8,128)(2,1)S(1)}, u32[]{:S(2)}, u32[]{:S(2)}) collective-permute-start(bf16[2,192,256]{2,1,0:T(8,128)(2,1)S(1)} %fusion.40), channel_id=1, source_target_pairs={{0,14},{2,0},{4,2},{6,4},{8,6},{10,8},{12,10},{14,12},{1,15},{3,1}... | collective-permute-start | bytes 589832 | tf_op jit(solution)/shard_map/ppermute | solution.py:33
  318.5 48.9 %collective-permute-start.48 = (bf16[112,3072]{1,0:T(8,128)(2,1)S(1)}, bf16[112,3072]{1,0:T(8,128)(2,1)S(1)}, u32[]{:S(2)}, u32[]{:S(2)}) collective-permute-start(bf16[112,3072]{1,0:T(8,128)(2,1)S(1)} %fusion.2), channel_id=1, source_target_pairs={{32,0},{64,32},{96,64},{128,96},{160,128},{192,160},{224,192},{33,... | collective-permute-start | bytes 2064392 | tf_op jit(solution)/shard_map/ppermute | solution.py:23
  321.1 41.3 %collective-permute-start.71 = (bf16[192,256]{1,0:T(8,128)(2,1)S(1)}, bf16[192,256]{1,0:T(8,128)(2,1)S(1)}, u32[]{:S(2)}, u32[]{:S(2)}) collective-permute-start(bf16[192,256]{1,0:T(8,128)(2,1)S(1)} %fusion.88), channel_id=1, source_target_pairs={{0,16},{16,0},{1,17},{17,1},{2,18},{18,2},{3,19},{19,3},{4,20},{20... | collective-permute-start | bytes 294920 | tf_op jit(solution)/shard_map/ppermute | solution.py:29
  324.3 43.2 %collective-permute-start.33 = (bf16[112,3072]{1,0:T(8,128)(2,1)S(1)}, bf16[112,3072]{1,0:T(8,128)(2,1)S(1)}, u32[]{:S(2)}, u32[]{:S(2)}) collective-permute-start(bf16[112,3072]{1,0:T(8,128)(2,1)S(1)} %fusion.1), channel_id=1, source_target_pairs={{0,32},{32,64},{64,96},{96,128},{128,160},{160,192},{192,224},{1,3... | collective-permute-start | bytes 2064392 | tf_op jit(solution)/shard_map/ppermute | solution.py:23
  (42 other events, 443.6 us)
